TPU v7x, 32 devices: a whole 2x2x4 slice. The times are simulated.
32 devices in a mesh: dp: 2 (over core), wide: 8 (over z, y), narrow: 2 (over x).
Axes of the slice: x: 2, y: 2, z: 4, core: 2. Of those that a mesh axis runs over, the one named last changes fastest.
Arguments:
- layer_input: bfloat16 [8192, 1088], P(('dp', 'wide'), 'narrow'), may hold values from -6 to 6
- doc_segments: int32 [2, 4096], replicated, may hold values from 0 to 7, as said below
- first_gain: bfloat16 [1088], P('narrow'), may hold values from 0.25 to 1.75
- first_shift: bfloat16 [1088], P('narrow'), may hold values from -2 to 2
- heads_weight: bfloat16 [1088, 3, 1088], P('narrow', None, 'wide'), may hold values from -1 to 1
- query_bias: bfloat16 [1088], P('wide'), may hold values from -2 to 2
- value_bias: bfloat16 [1088], P('wide'), may hold values from -2 to 2
- merge_weight: bfloat16 [1088, 1088], P('wide', 'narrow'), may hold values from -0.1875 to 0.1875
- merge_bias: bfloat16 [1088], P('narrow'), may hold values from -2 to 2
- second_gain: bfloat16 [1088], P('narrow'), may hold values from 0.25 to 1.75
- second_shift: bfloat16 [1088], P('narrow'), may hold values from -2 to 2
- up_weight: bfloat16 [1088, 4352], P('narrow', 'wide'), may hold values from -1 to 1
- up_bias: bfloat16 [4352], P('wide'), may hold values from -2 to 2
- down_weight: bfloat16 [4352, 1088], P('wide', 'narrow'), may hold values from -0.09375 to 0.09375
- down_bias: bfloat16 [1088], P('narrow'), may hold values from -2 to 2
- out_cotangent: bfloat16 [8192, 1088], P(('dp', 'wide'), 'narrow'), may hold values from -6 to 6
Outputs:
- layer_output: bfloat16 [8192, 1088], P(('dp', 'wide'), 'narrow')
- input_grad: bfloat16 [8192, 1088], P(('dp', 'wide'), 'narrow')
- first_gain_grad: float32 [1088], P('narrow')
- first_shift_grad: float32 [1088], P('narrow')
- heads_weight_grad: float32 [1088, 3, 1088], P('narrow', None, 'wide')
- query_bias_grad: float32 [1088], P('wide')
- value_bias_grad: float32 [1088], P('wide')
- merge_weight_grad: float32 [1088, 1088], P('wide', 'narrow')
- merge_bias_grad: float32 [1088], P('narrow')
- second_gain_grad: float32 [1088], P('narrow')
- second_shift_grad: float32 [1088], P('narrow')
- up_weight_grad: float32 [1088, 4352], P('narrow', 'wide')
- up_bias_grad: float32 [4352], P('wide')
- down_weight_grad: float32 [4352, 1088], P('wide', 'narrow')
- down_bias_grad: float32 [1088], P('narrow')
Inputs may be any that keep to these rules, and one draw needn't show every extreme that they name: `doc_segments`: in each sequence's row, numbers rise by one at each document's start and every number is used; each run of 4096 positions from the row's start holds 8 whole documents, three of them of exactly 1024 tokens, and no document is longer.
All inputs are finite; a program needn't handle non-finite values.
Results may differ from a plain program's by a relative error of at most 0.0228.
The roundings to bfloat16 on the way count: a program that leaves them out, or rounds other values in their place, can miss the bound.
Values may be sent and summed in bfloat16 or wider, within the bound.
A program may use at most 320 MiB of HBM per device.

v0:
```python
import jax
import jax.numpy as jnp
from jax import lax
from jax.sharding import PartitionSpec as P

HEAD = 64
REACH = 4


EPS = 1e-05
NEGATIVE = -1e30


def passed_along(shard, axis, by):
    count = lax.axis_size(axis)
    pairs = [(i, i + by) for i in range(count) if 0 <= i + by < count]
    return lax.ppermute(shard, axis, pairs)


def gelu_unit(values):
    return jax.nn.gelu(values, approximate=False)


def gelu_back(before, grad):
    _, back = jax.vjp(gelu_unit, before)
    return back(grad)[0]


def inner(left, right):
    return lax.dot_general(
        left, right, (((0,), (0,)), ((), ())), preferred_element_type=jnp.float32
    )


def inner_paired(natural, paired_rows):
    wide_count = lax.axis_size("wide")
    parts = lax.axis_size("narrow")
    tokens = natural.shape[0] // (wide_count * parts)
    left_view = natural.reshape(wide_count, parts, tokens, natural.shape[1])
    right_view = paired_rows.reshape(parts, wide_count, tokens, paired_rows.shape[1])
    return lax.dot_general(
        left_view,
        right_view,
        (((0, 1, 2), (1, 0, 2)), ((), ())),
        preferred_element_type=jnp.float32,
    )


def narrow_total(values):
    return lax.psum(values, "narrow")


def rows_wide(block):
    return lax.all_gather(block, "wide", axis=0, tiled=True)


def rows_narrow(block):
    return lax.all_gather(block, "narrow", axis=0, tiled=True)


def product_narrow(left, right, paired):
    parts = lax.axis_size("narrow")
    wide_count = lax.axis_size("wide")
    share = left.shape[0] // parts
    tokens = left.shape[0] // (wide_count * parts)

    def term(start, count):
        if paired:
            view = left.reshape(wide_count, parts, tokens, left.shape[1])
            piece = view
            piece = jnp.swapaxes(piece, 0, 1).reshape(count, left.shape[1])
        else:
            piece = left
        return jnp.dot(piece, right, preferred_element_type=jnp.float32)

    return lax.psum_scatter(
        term(jnp.int32(0), lax.axis_size("narrow") * share),
        "narrow",
        scatter_dimension=0,
        tiled=True,
    )


def product_wide(left, right, paired):
    parts = lax.axis_size("narrow")
    wide_count = lax.axis_size("wide")
    share = left.shape[0] // wide_count
    tokens = left.shape[0] // (wide_count * parts)

    def term(start, count):
        if paired:
            view = left.reshape(parts, wide_count, tokens, left.shape[1])
            piece = view
            piece = jnp.swapaxes(piece, 0, 1).reshape(count, left.shape[1])
        else:
            piece = left
        return jnp.dot(piece, right, preferred_element_type=jnp.float32)

    return lax.psum_scatter(
        term(jnp.int32(0), lax.axis_size("wide") * share), "wide", scatter_dimension=0, tiled=True
    )


def heads_in(block):
    return lax.all_to_all(block, "wide", split_axis=0, concat_axis=2, tiled=True)


def heads_out(block):
    return lax.all_to_all(block, "wide", split_axis=2, concat_axis=0, tiled=True)


def norm_forward(values, gain, shift, width):
    mean = narrow_total(jnp.sum(values, 1, keepdims=True)) / width
    centred = values - mean
    spread = narrow_total(jnp.sum(centred * centred, 1, keepdims=True)) / width
    scale = lax.rsqrt(spread + EPS)
    normed = centred * scale
    return (normed, scale, (normed * gain + shift).astype(jnp.bfloat16))


def norm_backward(grad, normed, scale, gain, width):
    scaled = grad * gain
    first, second = narrow_total(
        (jnp.sum(scaled, 1, keepdims=True), jnp.sum(scaled * normed, 1, keepdims=True))
    )
    back = scale * (scaled - first / width - normed * (second / width))
    return (back, jnp.sum(grad * normed, 0), jnp.sum(grad, 0))


def block_mask(segments, query_start, key_start, rows):
    places = jnp.arange(rows, dtype=jnp.int32)
    query_seg = lax.dynamic_slice_in_dim(segments, query_start, rows, 0)
    key_seg = lax.dynamic_slice_in_dim(segments, jnp.maximum(key_start, 0), rows, 0)
    key_pos = key_start + places
    query_pos = query_start + places
    same = query_seg[:, None] == key_seg[None, :]
    return same & (key_pos[None, :] <= query_pos[:, None]) & (key_pos[None, :] >= 0)


def scores(query, key, mask):
    raw = jnp.einsum("qhd,khd->hqk", query, key, preferred_element_type=jnp.float32) * HEAD ** (
        -0.5
    )
    return jnp.where(mask[None], raw, NEGATIVE)


def attend(query, keys, values, masks):
    top = None
    total = None
    for key, mask in zip(keys, masks):
        logits = scores(query, key, mask)
        block_top = jnp.max(logits, -1)
        if top is None:
            top = block_top
            total = jnp.sum(jnp.exp(logits - top[..., None]), -1)
        else:
            new_top = jnp.maximum(top, block_top)
            total = total * jnp.exp(top - new_top) + jnp.sum(
                jnp.exp(logits - new_top[..., None]), -1
            )
            top = new_top
    log_total = top + jnp.log(total)
    mixed = jnp.zeros(query.shape, jnp.float32)
    for key, value, mask in zip(keys, values, masks):
        probs = jnp.exp(scores(query, key, mask) - log_total[..., None]).astype(jnp.bfloat16)
        mixed = mixed + jnp.einsum("hqk,khd->qhd", probs, value, preferred_element_type=jnp.float32)
    return (mixed, log_total)


def attend_back(query, keys, values, masks, log_total, grad_out):
    delta = jnp.zeros(log_total.shape, jnp.float32)
    for key, value, mask in zip(keys, values, masks):
        probs = jnp.exp(scores(query, key, mask) - log_total[..., None])
        grad_probs = jnp.einsum("qhd,khd->hqk", grad_out, value, preferred_element_type=jnp.float32)
        delta = delta + jnp.sum(probs * grad_probs, -1)
    grad_query = jnp.zeros(query.shape, jnp.float32)
    key_grads = []
    value_grads = []
    factor = HEAD ** (-0.5)
    for key, value, mask in zip(keys, values, masks):
        probs = jnp.exp(scores(query, key, mask) - log_total[..., None])
        grad_probs = jnp.einsum("qhd,khd->hqk", grad_out, value, preferred_element_type=jnp.float32)
        grad_scores = (probs * (grad_probs - delta[..., None])).astype(jnp.bfloat16)
        grad_query = (
            grad_query
            + jnp.einsum("hqk,khd->qhd", grad_scores, key, preferred_element_type=jnp.float32)
            * factor
        )
        key_grads.append(
            jnp.einsum("hqk,qhd->khd", grad_scores, query, preferred_element_type=jnp.float32)
            * factor
        )
        value_grads.append(
            jnp.einsum(
                "hqk,qhd->khd",
                probs.astype(jnp.bfloat16),
                grad_out,
                preferred_element_type=jnp.float32,
            )
        )
    return (grad_query, key_grads, value_grads)


def shards(
    layer_input,
    doc_segments,
    first_gain,
    first_shift,
    heads_weight,
    query_bias,
    value_bias,
    merge_weight,
    merge_bias,
    second_gain,
    second_shift,
    up_weight,
    up_bias,
    down_weight,
    down_bias,
    out_cotangent,
):
    parts = lax.axis_size("narrow")
    width = layer_input.shape[1] * parts
    heads = width // HEAD
    cols = heads_weight.shape[2]
    half = heads_weight.shape[0]
    block_rows = layer_input.shape[0]
    rows = block_rows // parts
    weight_flat = heads_weight.reshape(half, 3 * cols)
    values_in = layer_input.astype(jnp.float32)
    gain_one = first_gain.astype(jnp.float32)
    gain_two = second_gain.astype(jnp.float32)
    normed1, scale1, low1 = norm_forward(
        values_in, gain_one, first_shift.astype(jnp.float32), width
    )
    low1_all = rows_wide(low1)
    projected = product_narrow(low1_all, weight_flat, True)
    bias_rows = jnp.stack(
        [
            query_bias.astype(jnp.float32),
            jnp.zeros((cols,), jnp.float32),
            value_bias.astype(jnp.float32),
        ]
    )
    packed = (projected.reshape(-1, 3, cols) + bias_rows[None]).astype(jnp.bfloat16)
    local = heads_in(packed)
    query = local[:, 0].reshape(rows, heads, HEAD)
    key_flat = local[:, 1]
    value_flat = local[:, 2]
    joined = lax.axis_index("wide") * parts + lax.axis_index("narrow")
    seg_row = lax.dynamic_index_in_dim(doc_segments, lax.axis_index("dp"), 0, keepdims=False)
    start = joined * rows
    keys = [key_flat.reshape(rows, heads, HEAD)]
    values = [value_flat.reshape(rows, heads, HEAD)]
    masks = [block_mask(seg_row, start, start, rows)]
    for back in range(1, REACH + 1):
        moved_key, moved_value = passed_along((key_flat, value_flat), ("wide", "narrow"), back)
        keys.append(moved_key.reshape(rows, heads, HEAD))
        values.append(moved_value.reshape(rows, heads, HEAD))
        masks.append(block_mask(seg_row, start, start - back * rows, rows))
    mixed, log_total = attend(query, keys, values, masks)
    mixed_low = mixed.astype(jnp.bfloat16).reshape(rows, width)
    mixed_blocks = heads_out(mixed_low.reshape(rows, 1, width))
    mixed_all = rows_narrow(mixed_blocks.reshape(mixed_blocks.shape[0], cols))
    branch = product_wide(mixed_all, merge_weight, True) + merge_bias.astype(jnp.float32)
    residual = values_in + branch
    normed2, scale2, low2 = norm_forward(
        residual, gain_two, second_shift.astype(jnp.float32), width
    )
    grad_out = out_cotangent.astype(jnp.float32)
    low2_all = rows_wide(low2)
    before = product_narrow(low2_all, up_weight, False) + up_bias.astype(jnp.float32)
    hidden = gelu_unit(before).astype(jnp.bfloat16)
    hidden_all = rows_narrow(hidden)
    result = residual + product_wide(hidden_all, down_weight, False) + down_bias.astype(jnp.float32)
    cotangent_all = rows_wide(out_cotangent)
    grad_hidden = product_narrow(cotangent_all, down_weight.T, False)
    grad_before = gelu_back(before, grad_hidden).astype(jnp.bfloat16)
    grad_before_all = rows_narrow(grad_before)
    up_grad = inner(low2_all, grad_before_all)
    up_bias_grad = jnp.sum(grad_before_all, 0, dtype=jnp.float32)
    down_grad = inner(hidden_all, cotangent_all)
    grad_low2 = product_wide(grad_before_all, up_weight.T, False)
    layer_output = result.astype(jnp.bfloat16)
    down_bias_part = jnp.sum(grad_out, 0)
    grad_norm2, second_gain_part, second_shift_part = norm_backward(
        grad_low2, normed2, scale2, gain_two, width
    )
    grad_residual = grad_out + grad_norm2
    grad_branch = grad_residual.astype(jnp.bfloat16)
    merge_bias_part = jnp.sum(grad_branch, 0, dtype=jnp.float32)
    branch_all = rows_wide(grad_branch)
    merge_grad = inner_paired(branch_all, mixed_all).T
    grad_mixed = product_narrow(branch_all, merge_weight.T, True).astype(jnp.bfloat16)
    grad_attn = heads_in(grad_mixed.reshape(grad_mixed.shape[0], 1, cols)).reshape(
        rows, heads, HEAD
    )
    grad_query, key_grads, value_grads = attend_back(
        query, keys, values, masks, log_total, grad_attn
    )
    key_total = key_grads[0].reshape(rows, width)
    value_total = value_grads[0].reshape(rows, width)
    for back in range(1, REACH + 1):
        key_in, value_in = (
            passed_along(
                key_grads[back].reshape(rows, width).astype(jnp.bfloat16), ("wide", "narrow"), -back
            ).astype(jnp.float32),
            passed_along(
                value_grads[back].reshape(rows, width).astype(jnp.bfloat16),
                ("wide", "narrow"),
                -back,
            ).astype(jnp.float32),
        )
        key_total = key_total + key_in
        value_total = value_total + value_in
    grad_heads = jnp.stack([grad_query.reshape(rows, width), key_total, value_total], 1).astype(
        jnp.bfloat16
    )
    grad_packed = heads_out(grad_heads)
    grad_packed_all = rows_narrow(grad_packed.reshape(grad_packed.shape[0], 3 * cols))
    heads_grad = inner_paired(low1_all, grad_packed_all).reshape(half, 3, cols)
    column_sums = jnp.sum(grad_packed_all, 0, dtype=jnp.float32).reshape(3, cols)
    query_grad = column_sums[0]
    value_grad = column_sums[2]
    grad_low1 = product_wide(grad_packed_all, weight_flat.T, True)
    grad_norm1, first_gain_part, first_shift_part = norm_backward(
        grad_low1, normed1, scale1, gain_one, width
    )
    input_grad = (grad_residual + grad_norm1).astype(jnp.bfloat16)
    heads_total, query_total, value_bias_total, merge_total, up_total, up_bias_total, down_total = (
        lax.psum(heads_grad.astype(jnp.bfloat16), "dp").astype(jnp.float32),
        lax.psum(query_grad.astype(jnp.bfloat16), "dp").astype(jnp.float32),
        lax.psum(value_grad.astype(jnp.bfloat16), "dp").astype(jnp.float32),
        lax.psum(merge_grad.astype(jnp.bfloat16), "dp").astype(jnp.float32),
        lax.psum(up_grad.astype(jnp.bfloat16), "dp").astype(jnp.float32),
        lax.psum(up_bias_grad.astype(jnp.bfloat16), "dp").astype(jnp.float32),
        lax.psum(down_grad.astype(jnp.bfloat16), "dp").astype(jnp.float32),
    )
    (
        first_gain_total,
        first_shift_total,
        merge_bias_total,
        second_gain_total,
        second_shift_total,
        down_bias_total,
    ) = lax.psum(
        (
            first_gain_part,
            first_shift_part,
            merge_bias_part,
            second_gain_part,
            second_shift_part,
            down_bias_part,
        ),
        ("dp", "wide"),
    )
    return (
        layer_output,
        input_grad,
        first_gain_total,
        first_shift_total,
        heads_total,
        query_total,
        value_bias_total,
        merge_total,
        merge_bias_total,
        second_gain_total,
        second_shift_total,
        up_total,
        up_bias_total,
        down_total,
        down_bias_total,
    )


def solution(mesh):
    return jax.shard_map(
        shards,
        mesh=mesh,
        in_specs=(
            P(("dp", "wide"), "narrow"),
            P(),
            P("narrow"),
            P("narrow"),
            P("narrow", None, "wide"),
            P("wide"),
            P("wide"),
            P("wide", "narrow"),
            P("narrow"),
            P("narrow"),
            P("narrow"),
            P("narrow", "wide"),
            P("wide"),
            P("wide", "narrow"),
            P("narrow"),
            P(("dp", "wide"), "narrow"),
        ),
        out_specs=(
            P(("dp", "wide"), "narrow"),
            P(("dp", "wide"), "narrow"),
            P("narrow"),
            P("narrow"),
            P("narrow", None, "wide"),
            P("wide"),
            P("wide"),
            P("wide", "narrow"),
            P("narrow"),
            P("narrow"),
            P("narrow"),
            P("narrow", "wide"),
            P("wide"),
            P("wide", "narrow"),
            P("narrow"),
        ),
        check_vma=False,
    )
```

profile of v0, /device:TPU:11, one launch (start us, length us, event | category | flops | bytes accessed | tf_op | source)
XLA Modules:
  0.0 2102.4 jit_solution(8123056806612442823)
XLA Ops:
  20.9 79.3 %all-gather.9.cloned.1.call-done = bf16[4096,544]{0,1:T(8,128)(2,1)} async-done(((bf16[512,544]{0,1:T(8,128)(2,1)}), bf16[4096,544]{0,1:T(8,128)(2,1)}) %all-gather.9.cloned.1.call-update) | async-done | bytes 4456464 | tf_op jit(solution)/shard_map/all_gather | solution.py:54
  100.2 11.1 reshape.642
  117.5 4.7 fusion.115
  123.0 80.2 %reduce-scatter.9.cloned.1.call-done = f32[2048,408]{0,1:T(8,128)} async-done(((f32[4096,408]{0,1:T(8,128)}), f32[2048,408]{0,1:T(8,128)}) %reduce-scatter.9.cloned.1.call-update) | async-done | bytes 3342352 | tf_op jit(solution)/shard_map/reduce_scatter | solution.py:76
  205.4 4.7 copy.193
  210.1 8.6 reshape.672
  218.7 5.5 all-to-all-start
  226.0 35.5 %all-to-all-done = bf16[8,2,52224]{2,1,0:T(2,128)(2,1)S(1)} async-done(((bf16[8,2,52224]{2,1,0:T(2,128)(2,1)}), bf16[8,2,52224]{2,1,0:T(2,128)(2,1)S(1)}, u32[]{:S(2)}, u32[]{:S(2)}) %all-to-all-start) | async-done | bytes 1671200 | tf_op jit(solution)/shard_map/all_to_all | solution.py:105
  261.5 6.7 reshape.673
  268.1 6.8 copy.194
  278.5 6.1 collective-permute-start.6
  294.3 21.2 %collective-permute-done = bf16[256,1088]{0,1:T(8,128)(2,1)S(1)} collective-permute-done((bf16[256,1088]{0,1:T(8,128)(2,1)S(1)}, bf16[256,1088]{0,1:T(8,128)(2,1)S(1)}, u32[]{:S(2)}, u32[]{:S(2)}) %collective-permute-start) | collective-permute-done | bytes 557088 | tf_op jit(solution)/shard_map/ppermute | solution.py:17
  315.4 27.6 %collective-permute-start.2 = (bf16[256,1088]{0,1:T(8,128)(2,1)S(1)}, bf16[256,1088]{0,1:T(8,128)(2,1)S(1)}, u32[]{:S(2)}, u32[]{:S(2)}) collective-permute-start(bf16[256,1088]{0,1:T(8,128)(2,1)S(1)} %get-tuple-element.57), channel_id=1, source_target_pairs={{0,3},{1,4},{2,5},{3,6},{4,7},{5,8},{6,9},{7,10},{8,11},{9,12},{10... | collective-permute-start | bytes 1671176 | tf_op jit(solution)/shard_map/ppermute | solution.py:17
  344.0 6.0 collective-permute-start.3
  356.4 10.7 collective-permute-done.3
  378.8 6.5 copy.284
  385.8 5.9 reduce.2
  391.9 20.1 all_to_all.63
  413.5 22.1 %all-gather.11.cloned.1.call-done = bf16[4096,136]{0,1:T(8,128)(2,1)} async-done(((bf16[2048,136]{0,1:T(8,128)(2,1)}), bf16[4096,136]{0,1:T(8,128)(2,1)}) %all-gather.11.cloned.1.call-update) | async-done | bytes 1114128 | tf_op jit(solution)/shard_map/all_gather | solution.py:58
  443.1 5.8 fusion.116
  449.6 155.4 %reduce-scatter.11.cloned.1.call-done = f32[512,544]{0,1:T(8,128)} async-done(((f32[4096,544]{0,1:T(8,128)}), f32[512,544]{0,1:T(8,128)}) %reduce-scatter.11.cloned.1.call-update) | async-done | bytes 1114128 | tf_op jit(solution)/shard_map/reduce_scatter | solution.py:99
  615.4 68.0 %all-gather.17.cloned.1.call-done = bf16[4096,544]{0,1:T(8,128)(2,1)} async-done(((bf16[512,544]{0,1:T(8,128)(2,1)}), bf16[4096,544]{0,1:T(8,128)(2,1)}) %all-gather.17.cloned.1.call-update) | async-done | bytes 4456464 | tf_op jit(solution)/shard_map/all_gather | solution.py:54
  683.3 9.6 fusion.128
  693.2 69.1 %all-gather.13.cloned.1.call-done = bf16[4096,544]{0,1:T(8,128)(2,1)} async-done(((bf16[512,544]{0,1:T(8,128)(2,1)}), bf16[4096,544]{0,1:T(8,128)(2,1)}) %all-gather.13.cloned.1.call-update) | async-done | bytes 4456464 | tf_op jit(solution)/shard_map/all_gather | solution.py:54
  762.2 9.4 fusion.117
  772.3 96.8 %reduce-scatter.17.cloned.1.call-done = f32[2048,544]{0,1:T(8,128)} async-done(((f32[4096,544]{0,1:T(8,128)}), f32[2048,544]{0,1:T(8,128)}) %reduce-scatter.17.cloned.1.call-update) | async-done | bytes 4456464 | tf_op jit(solution)/shard_map/reduce_scatter | solution.py:76
  869.1 107.3 %reduce-scatter.13.cloned.1.call-done = f32[2048,544]{0,1:T(8,128)} async-done(((f32[4096,544]{0,1:T(8,128)}), f32[2048,544]{0,1:T(8,128)}) %reduce-scatter.13.cloned.1.call-update) | async-done | bytes 4456464 | tf_op jit(solution)/shard_map/reduce_scatter | solution.py:76
  976.4 13.6 add_convert_fusion
  990.2 59.8 %all-gather.19.cloned.1.call-done = bf16[4096,544]{0,1:T(8,128)(2,1)} async-done(((bf16[2048,544]{0,1:T(8,128)(2,1)}), bf16[4096,544]{0,1:T(8,128)(2,1)}) %all-gather.19.cloned.1.call-update) | async-done | bytes 4456464 | tf_op jit(solution)/shard_map/all_gather | solution.py:58
  1050.0 8.2 fusion.129
  1058.2 156.2 %reduce-scatter.19.cloned.1.call-done = f32[512,544]{0,1:T(8,128)} async-done(((f32[4096,544]{0,1:T(8,128)}), f32[512,544]{0,1:T(8,128)}) %reduce-scatter.19.cloned.1.call-update) | async-done | bytes 1114128 | tf_op jit(solution)/shard_map/reduce_scatter | solution.py:99
  1223.1 77.1 %all-gather.21.cloned.1.call-done = bf16[4096,544]{0,1:T(8,128)(2,1)} async-done(((bf16[512,544]{0,1:T(8,128)(2,1)}), bf16[4096,544]{0,1:T(8,128)(2,1)}) %all-gather.21.cloned.1.call-update) | async-done | bytes 4456464 | tf_op jit(solution)/shard_map/all_gather | solution.py:54
  1300.2 11.1 reshape.657
  1319.9 32.9 %reduce-scatter.21.cloned.1.call-done = f32[2048,136]{0,1:T(8,128)} async-done(((f32[4096,136]{0,1:T(8,128)}), f32[2048,136]{0,1:T(8,128)}) %reduce-scatter.21.cloned.1.call-update) | async-done | bytes 1114128 | tf_op jit(solution)/shard_map/reduce_scatter | solution.py:76
  1358.8 5.5 all-to-all-start.2
  1364.3 5.6 multiply_convert_fusion.5
  1370.1 5.9 all-to-all-done.2
  1376.0 4.9 reshape.677
  1381.0 4.6 copy.205
  1385.8 4.3 convolution_convert_fusion.2
  1411.9 17.1 multiply_reduce_fusion.3
  1429.0 21.1 %multiply_convert_fusion.3 = (bf16[17,256,256]{1,2,0:T(8,128)(2,1)}, bf16[17,256,256]{1,2,0:T(8,128)(2,1)}, bf16[17,256,256]{1,2,0:T(8,128)(2,1)}, bf16[17,256,256]{1,2,0:T(8,128)(2,1)}, bf16[17,256,256]{1,2,0:T(8,128)(2,1)}) fusion(f32[17,256,256]{1,2,0:T(8,128)} %get-tuple-element.91, f32[17,256,256]{1,2,0:T(8,128)} %copy-done.2, ...), kind=kLoop, calls=%fused_computation.10 | loop fusion | flops 33423360 | bytes 56068096 | tf_op jit(solution)/shard_map/convert_element_type | solution.py:183
  1458.1 5.7 collective-permute-start.13
  1475.1 5.4 collective-permute-done.12
  1480.6 4.9 collective-permute-start.10
  1489.2 17.6 collective-permute-done.14
  1508.7 4.7 collective-permute-done.15
  1513.8 11.6 collective-permute-done.11
  1525.4 17.2 collective-permute-done.10
  1542.6 5.1 collective-permute-done.9
  1548.3 8.6 copy.222
  1556.9 71.6 %all_to_all.64 = bf16[256,3,1088]{0,1,2:T(4,128)(2,1)S(1)} all-to-all(bf16[256,3,1088]{0,1,2:T(4,128)(2,1)S(1)} %copy.222), channel_id=1, replica_groups=mesh['dp'=2,'wide'=8,'narrow'=2] {'wide'}, dimensions={2} | all-to-all | bytes 3342336 | tf_op jit(solution)/shard_map/all_to_all | solution.py:109
  1631.3 8.1 convolution_convert_fusion.1
  1639.4 9.0 convolution_convert_fusion
  1648.5 6.1 fusion.52
  1654.6 23.3 %all-gather.23.cloned.1.call-done = bf16[4096,408]{0,1:T(8,128)(2,1)} async-done(((bf16[2048,408]{0,1:T(8,128)(2,1)}), bf16[4096,408]{0,1:T(8,128)(2,1)}) %all-gather.23.cloned.1.call-update) | async-done | bytes 3342352 | tf_op jit(solution)/shard_map/all_gather | solution.py:58
  1682.6 8.3 fusion.44
  1691.0 7.1 copy.225
  1698.1 8.6 reshape.665
  1706.8 7.9 fusion.127
  1715.8 9.4 fusion.118
  1743.7 130.1 %reduce-scatter.23.cloned.1.call-done = f32[512,544]{0,1:T(8,128)} async-done(((f32[4096,544]{0,1:T(8,128)}), f32[512,544]{0,1:T(8,128)}) %reduce-scatter.23.cloned.1.call-update) | async-done | bytes 1114128 | tf_op jit(solution)/shard_map/reduce_scatter | solution.py:99
  1879.4 154.0 %reduce-scatter.15.cloned.1.call-done = f32[512,544]{0,1:T(8,128)} async-done(((f32[4096,544]{0,1:T(8,128)}), f32[512,544]{0,1:T(8,128)}) %reduce-scatter.15.cloned.1.call-update) | async-done | bytes 1114128 | tf_op jit(solution)/shard_map/reduce_scatter | solution.py:99
  2037.2 58.5 %all-reduce = (f32[544]{0:T(1024)}, f32[544]{0:T(1024)}, f32[544]{0:T(1024)}, f32[544]{0:T(1024)}, f32[544]{0:T(1024)}, /*index=5*/f32[544]{0:T(1024)}) all-reduce(f32[544]{0:T(1024)S(1)} %get-tuple-element.17, f32[544]{0:T(1024)S(1)} %get-tuple-element.22, ...), channel_id=1, replica_groups=mesh['dp'=2,'wide'=8,'narrow'=2] {'dp','wide'}, use_global_device_ids=true, to_apply=%region_40.41 | all-reduce | flops 3264 | bytes 26112 | tf_op jit(solution)/shard_map/psum | solution.py:346
  (309 shorter events, 185.4 us)
Async XLA Ops:
  7.2 755.1 %copy-start = (bf16[544,544]{1,0:T(8,128)(2,1)S(1)}, bf16[544,544]{1,0:T(8,128)(2,1)}, u32[]{:S(2)}) copy-start(bf16[544,544]{1,0:T(8,128)(2,1)} %param.27) | copy-start | bytes 1775620
  7.2 93.0 %all-gather.9.cloned.1.call-start = ((), (), s32[]{:S(2)}) async-start(), calls=%async_computation.12 | async-start | bytes 5013504 | tf_op jit(solution)/shard_map/all_gather | solution.py:54
  12.3 99.0 %copy-start.46 = (f32[512,1]{0,1:T(1,128)}, f32[512,1]{0,1:T(1,128)S(1)}, u32[]{:S(2)}) copy-start(f32[512,1]{0,1:T(1,128)S(1)} %broadcast_multiply_fusion.5) | copy-start | bytes 6148
  20.8 182.4 %reduce-scatter.9.cloned.1.call-start = ((), (), s32[]{:S(2)}) async-start(), calls=%async_computation.13 | async-start | bytes 10027008 | tf_op jit(solution)/shard_map/reduce_scatter | solution.py:76
  218.7 42.8 %all-to-all-start = ((bf16[8,2,52224]{2,1,0:T(2,128)(2,1)}), bf16[8,2,52224]{2,1,0:T(2,128)(2,1)S(1)}, u32[]{:S(2)}, u32[]{:S(2)}) async-start(bf16[8,2,52224]{2,1,0:T(2,128)(2,1)} %reshape.672), calls=%async_computation.1 | async-start | bytes 3342336 | tf_op jit(solution)/shard_map/all_to_all | solution.py:105
  224.2 211.4 %all-gather.11.cloned.1.call-start = ((), (), s32[]{:S(2)}) async-start(), calls=%async_computation.14 | async-start | bytes 1671168 | tf_op jit(solution)/shard_map/all_gather | solution.py:58
  276.5 15.9 copy-start.19
  276.6 98.7 %copy-start.27 = (bf16[256,1,1088]{0,2,1:T(8,128)(2,1)}, bf16[256,1,1088]{0,2,1:T(8,128)(2,1)S(1)}, u32[]{:S(2)}) copy-start(bf16[256,1,1088]{0,2,1:T(8,128)(2,1)S(1)} %get-tuple-element.55) | copy-start | bytes 1671172
  276.6 96.5 %collective-permute-start.7 = (bf16[256,1088]{0,1:T(8,128)(2,1)S(1)}, bf16[256,1088]{0,1:T(8,128)(2,1)S(1)}, u32[]{:S(2)}, u32[]{:S(2)}) collective-permute-start(bf16[256,1088]{0,1:T(8,128)(2,1)S(1)} %get-tuple-element.56), channel_id=1, source_target_pairs={{0,4},{1,5},{2,6},{3,7},{4,8},{5,9},{6,10},{7,11},{8,12},{9,13},{1... | collective-permute-start | bytes 1671176 | tf_op jit(solution)/shard_map/ppermute | solution.py:17
  278.5 95.7 %collective-permute-start.6 = (bf16[256,1088]{0,1:T(8,128)(2,1)S(1)}, bf16[256,1088]{0,1:T(8,128)(2,1)S(1)}, u32[]{:S(2)}, u32[]{:S(2)}) collective-permute-start(bf16[256,1088]{0,1:T(8,128)(2,1)S(1)} %get-tuple-element.56), channel_id=1, source_target_pairs={{0,3},{1,4},{2,5},{3,6},{4,7},{5,8},{6,9},{7,10},{8,11},{9,12},{10... | collective-permute-start | bytes 1671176 | tf_op jit(solution)/shard_map/ppermute | solution.py:17
  284.6 93.0 %collective-permute-start.5 = (bf16[256,1088]{0,1:T(8,128)(2,1)S(1)}, bf16[256,1088]{0,1:T(8,128)(2,1)S(1)}, u32[]{:S(2)}, u32[]{:S(2)}) collective-permute-start(bf16[256,1088]{0,1:T(8,128)(2,1)S(1)} %get-tuple-element.56), channel_id=1, source_target_pairs={{0,2},{1,3},{2,4},{3,5},{4,6},{5,7},{6,8},{7,9},{8,10},{9,11},{10,... | collective-permute-start | bytes 1671176 | tf_op jit(solution)/shard_map/ppermute | solution.py:17
  287.0 57.0 %collective-permute-start.1 = (bf16[256,1088]{0,1:T(8,128)(2,1)S(1)}, bf16[256,1088]{0,1:T(8,128)(2,1)S(1)}, u32[]{:S(2)}, u32[]{:S(2)}) collective-permute-start(bf16[256,1088]{0,1:T(8,128)(2,1)S(1)} %get-tuple-element.57), channel_id=1, source_target_pairs={{0,2},{1,3},{2,4},{3,5},{4,6},{5,7},{6,8},{7,9},{8,10},{9,11},{10,... | collective-permute-start | bytes 1671176 | tf_op jit(solution)/shard_map/ppermute | solution.py:17
  289.0 26.4 %collective-permute-start = (bf16[256,1088]{0,1:T(8,128)(2,1)S(1)}, bf16[256,1088]{0,1:T(8,128)(2,1)S(1)}, u32[]{:S(2)}, u32[]{:S(2)}) collective-permute-start(bf16[256,1088]{0,1:T(8,128)(2,1)S(1)} %get-tuple-element.57), channel_id=1, source_target_pairs={{0,1},{1,2},{2,3},{3,4},{4,5},{5,6},{6,7},{7,8},{8,9},{9,10},{10,1... | collective-permute-start | bytes 1671176 | tf_op jit(solution)/shard_map/ppermute | solution.py:17
  293.3 82.0 %copy-start.4 = (f32[17,256,256]{1,2,0:T(8,128)}, f32[17,256,256]{1,2,0:T(8,128)S(1)}, u32[]{:S(2)}) copy-start(f32[17,256,256]{1,2,0:T(8,128)S(1)} %get-tuple-element.88) | copy-start | bytes 13369348
  315.4 35.5 %copy-start.25 = (bf16[256,1088]{0,1:T(8,128)(2,1)}, bf16[256,1088]{0,1:T(8,128)(2,1)S(1)}, u32[]{:S(2)}) copy-start(bf16[256,1088]{0,1:T(8,128)(2,1)S(1)} %collective-permute-done) | copy-start | bytes 1671172
  315.4 37.1 %collective-permute-start.2 = (bf16[256,1088]{0,1:T(8,128)(2,1)S(1)}, bf16[256,1088]{0,1:T(8,128)(2,1)S(1)}, u32[]{:S(2)}, u32[]{:S(2)}) collective-permute-start(bf16[256,1088]{0,1:T(8,128)(2,1)S(1)} %get-tuple-element.57), channel_id=1, source_target_pairs={{0,3},{1,4},{2,5},{3,6},{4,7},{5,8},{6,9},{7,10},{8,11},{9,12},{10... | collective-permute-start | bytes 1671176 | tf_op jit(solution)/shard_map/ppermute | solution.py:17
  344.0 32.5 %copy-start.2 = (f32[17,256,256]{1,2,0:T(8,128)}, f32[17,256,256]{1,2,0:T(8,128)S(1)}, u32[]{:S(2)}) copy-start(f32[17,256,256]{1,2,0:T(8,128)S(1)} %get-tuple-element.90) | copy-start | bytes 13369348
  344.0 12.4 copy-start.23
  344.0 23.2 %collective-permute-start.3 = (bf16[256,1088]{0,1:T(8,128)(2,1)S(1)}, bf16[256,1088]{0,1:T(8,128)(2,1)S(1)}, u32[]{:S(2)}, u32[]{:S(2)}) collective-permute-start(bf16[256,1088]{0,1:T(8,128)(2,1)S(1)} %get-tuple-element.57), channel_id=1, source_target_pairs={{0,4},{1,5},{2,6},{3,7},{4,8},{5,9},{6,10},{7,11},{8,12},{9,13},{1... | collective-permute-start | bytes 1671176 | tf_op jit(solution)/shard_map/ppermute | solution.py:17
  350.9 26.7 %copy-start.3 = (f32[17,256,256]{1,2,0:T(8,128)}, f32[17,256,256]{1,2,0:T(8,128)S(1)}, u32[]{:S(2)}) copy-start(f32[17,256,256]{1,2,0:T(8,128)S(1)} %get-tuple-element.86) | copy-start | bytes 13369348
  352.6 14.6 copy-start.31
  352.6 23.8 %collective-permute-start.4 = (bf16[256,1088]{0,1:T(8,128)(2,1)S(1)}, bf16[256,1088]{0,1:T(8,128)(2,1)S(1)}, u32[]{:S(2)}, u32[]{:S(2)}) collective-permute-start(bf16[256,1088]{0,1:T(8,128)(2,1)S(1)} %get-tuple-element.56), channel_id=1, source_target_pairs={{0,1},{1,2},{2,3},{3,4},{4,5},{5,6},{6,7},{7,8},{8,9},{9,10},{10,1... | collective-permute-start | bytes 1671176 | tf_op jit(solution)/shard_map/ppermute | solution.py:17
  356.4 17.8 copy-start.5
  413.5 191.5 %reduce-scatter.11.cloned.1.call-start = ((), (), s32[]{:S(2)}) async-start(), calls=%async_computation.15 | async-start | bytes 10027008 | tf_op jit(solution)/shard_map/reduce_scatter | solution.py:99
  448.9 156.1 %copy-start.14 = (bf16[512,544]{0,1:T(8,128)(2,1)S(1)}, bf16[512,544]{0,1:T(8,128)(2,1)}, u32[]{:S(2)}) copy-start(bf16[512,544]{0,1:T(8,128)(2,1)} %param.16) | copy-start | bytes 1671172
  448.9 234.5 %all-gather.17.cloned.1.call-start = ((), (), s32[]{:S(2)}) async-start(), calls=%async_computation.20 | async-start | bytes 5013504 | tf_op jit(solution)/shard_map/all_gather | solution.py:54
  449.5 312.8 %all-gather.13.cloned.1.call-start = ((), (), s32[]{:S(2)}) async-start(), calls=%async_computation.16 | async-start | bytes 5013504 | tf_op jit(solution)/shard_map/all_gather | solution.py:54
  606.5 613.6 %copy-start.7 = (f32[512,544]{0,1:T(8,128)}, f32[512,544]{0,1:T(8,128)S(1)}, u32[]{:S(2)}) copy-start(f32[512,544]{0,1:T(8,128)S(1)} %get-tuple-element.50) | copy-start | bytes 3342340
  615.3 253.8 %reduce-scatter.17.cloned.1.call-start = ((), (), s32[]{:S(2)}) async-start(), calls=%async_computation.21 | async-start | bytes 13369344 | tf_op jit(solution)/shard_map/reduce_scatter | solution.py:76
  692.9 283.5 %reduce-scatter.13.cloned.1.call-start = ((), (), s32[]{:S(2)}) async-start(), calls=%async_computation.17 | async-start | bytes 13369344 | tf_op jit(solution)/shard_map/reduce_scatter | solution.py:76
  771.7 278.3 %all-gather.19.cloned.1.call-start = ((), (), s32[]{:S(2)}) async-start(), calls=%async_computation.22 | async-start | bytes 6684672 | tf_op jit(solution)/shard_map/all_gather | solution.py:58
  990.1 224.3 %reduce-scatter.19.cloned.1.call-start = ((), (), s32[]{:S(2)}) async-start(), calls=%async_computation.23 | async-start | bytes 10027008 | tf_op jit(solution)/shard_map/reduce_scatter | solution.py:99
  1058.2 161.9 %copy-start.18 = (bf16[512,544]{0,1:T(8,128)(2,1)S(1)}, bf16[512,544]{0,1:T(8,128)(2,1)}, u32[]{:S(2)}) copy-start(bf16[512,544]{0,1:T(8,128)(2,1)} %param.31) | copy-start | bytes 1671172
  1058.2 242.0 %all-gather.21.cloned.1.call-start = ((), (), s32[]{:S(2)}) async-start(), calls=%async_computation.24 | async-start | bytes 5013504 | tf_op jit(solution)/shard_map/all_gather | solution.py:54
  1222.6 130.2 %reduce-scatter.21.cloned.1.call-start = ((), (), s32[]{:S(2)}) async-start(), calls=%async_computation.25 | async-start | bytes 3342336 | tf_op jit(solution)/shard_map/reduce_scatter | solution.py:76
  1358.8 17.2 all-to-all-start.2
  1364.3 275.1 %all-gather.15.cloned.1.call-start = ((), (), s32[]{:S(2)}) async-start(), calls=%async_computation.18 | async-start | bytes 6684672 | tf_op jit(solution)/shard_map/all_gather | solution.py:58
  1369.9 308.0 %all-gather.23.cloned.1.call-start = ((), (), s32[]{:S(2)}) async-start(), calls=%async_computation.26 | async-start | bytes 5013504 | tf_op jit(solution)/shard_map/all_gather | solution.py:58
  1385.8 12.7 slice-start
  1429.0 23.7 %copy-start.34 = (bf16[256,1088]{0,1:T(8,128)(2,1)S(1)}, bf16[256,1088]{0,1:T(8,128)(2,1)}, u32[]{:S(2)}) copy-start(bf16[256,1088]{0,1:T(8,128)(2,1)} %copy-done.33) | copy-start | bytes 1671172
  1453.2 10.5 copy-start.57
  1453.3 12.5 copy-start.56
  1453.3 14.4 copy-start.11
  1454.1 14.4 copy-start.10
  1454.1 15.2 copy-start.9
  1454.1 15.2 copy-start.32
  1454.7 25.9 %collective-permute-start.12 = (bf16[256,1088]{0,1:T(8,128)(2,1)S(1)}, bf16[256,1088]{0,1:T(8,128)(2,1)S(1)}, u32[]{:S(2)}, u32[]{:S(2)}) collective-permute-start(bf16[256,1088]{0,1:T(8,128)(2,1)S(1)} %bitcast.379), channel_id=1, source_target_pairs={{1,0},{2,1},{3,2},{4,3},{5,4},{6,5},{7,6},{8,7},{9,8},{10,9},{11,1... | collective-permute-start | bytes 1671176 | tf_op jit(solution)/shard_map/ppermute | solution.py:17
  1458.1 27.4 %collective-permute-start.13 = (bf16[256,1088]{0,1:T(8,128)(2,1)S(1)}, bf16[256,1088]{0,1:T(8,128)(2,1)S(1)}, u32[]{:S(2)}, u32[]{:S(2)}) collective-permute-start(bf16[256,1088]{0,1:T(8,128)(2,1)S(1)} %bitcast.378), channel_id=1, source_target_pairs={{2,0},{3,1},{4,2},{5,3},{6,4},{7,5},{8,6},{9,7},{10,8},{11,9},{12,... | collective-permute-start | bytes 1671176 | tf_op jit(solution)/shard_map/ppermute | solution.py:17
  1463.8 43.0 %collective-permute-start.14 = (bf16[256,1088]{0,1:T(8,128)(2,1)S(1)}, bf16[256,1088]{0,1:T(8,128)(2,1)S(1)}, u32[]{:S(2)}, u32[]{:S(2)}) collective-permute-start(bf16[256,1088]{0,1:T(8,128)(2,1)S(1)} %bitcast.377), channel_id=1, source_target_pairs={{3,0},{4,1},{5,2},{6,3},{7,4},{8,5},{9,6},{10,7},{11,8},{12,9},{13... | collective-permute-start | bytes 1671176 | tf_op jit(solution)/shard_map/ppermute | solution.py:17
  1465.7 47.7 %collective-permute-start.15 = (bf16[256,1088]{0,1:T(8,128)(2,1)S(1)}, bf16[256,1088]{0,1:T(8,128)(2,1)S(1)}, u32[]{:S(2)}, u32[]{:S(2)}) collective-permute-start(bf16[256,1088]{0,1:T(8,128)(2,1)S(1)} %bitcast.376), channel_id=1, source_target_pairs={{4,0},{5,1},{6,2},{7,3},{8,4},{9,5},{10,6},{11,7},{12,8},{13,9},{1... | collective-permute-start | bytes 1671176 | tf_op jit(solution)/shard_map/ppermute | solution.py:17
  1470.4 55.0 %collective-permute-start.11 = (bf16[256,1088]{0,1:T(8,128)(2,1)S(1)}, bf16[256,1088]{0,1:T(8,128)(2,1)S(1)}, u32[]{:S(2)}, u32[]{:S(2)}) collective-permute-start(bf16[256,1088]{0,1:T(8,128)(2,1)S(1)} %bitcast.328), channel_id=1, source_target_pairs={{4,0},{5,1},{6,2},{7,3},{8,4},{9,5},{10,6},{11,7},{12,8},{13,9},{1... | collective-permute-start | bytes 1671176 | tf_op jit(solution)/shard_map/ppermute | solution.py:17
  1480.6 62.1 %collective-permute-start.10 = (bf16[256,1088]{0,1:T(8,128)(2,1)S(1)}, bf16[256,1088]{0,1:T(8,128)(2,1)S(1)}, u32[]{:S(2)}, u32[]{:S(2)}) collective-permute-start(bf16[256,1088]{0,1:T(8,128)(2,1)S(1)} %bitcast.331), channel_id=1, source_target_pairs={{3,0},{4,1},{5,2},{6,3},{7,4},{8,5},{9,6},{10,7},{11,8},{12,9},{13... | collective-permute-start | bytes 1671176 | tf_op jit(solution)/shard_map/ppermute | solution.py:17
  1485.5 62.2 %collective-permute-start.9 = (bf16[256,1088]{0,1:T(8,128)(2,1)S(1)}, bf16[256,1088]{0,1:T(8,128)(2,1)S(1)}, u32[]{:S(2)}, u32[]{:S(2)}) collective-permute-start(bf16[256,1088]{0,1:T(8,128)(2,1)S(1)} %bitcast.330), channel_id=1, source_target_pairs={{2,0},{3,1},{4,2},{5,3},{6,4},{7,5},{8,6},{9,7},{10,8},{11,9},{12,... | collective-permute-start | bytes 1671176 | tf_op jit(solution)/shard_map/ppermute | solution.py:17
  1506.8 40.9 %collective-permute-start.8 = (bf16[256,1088]{0,1:T(8,128)(2,1)S(1)}, bf16[256,1088]{0,1:T(8,128)(2,1)S(1)}, u32[]{:S(2)}, u32[]{:S(2)}) collective-permute-start(bf16[256,1088]{0,1:T(8,128)(2,1)S(1)} %bitcast.329), channel_id=1, source_target_pairs={{1,0},{2,1},{3,2},{4,3},{5,4},{6,5},{7,6},{8,7},{9,8},{10,9},{11,1... | collective-permute-start | bytes 1671176 | tf_op jit(solution)/shard_map/ppermute | solution.py:17
  1630.8 105.5 %all-reduce.7.cloned.1.call-start = ((), (), s32[]{:S(2)}) async-start(), calls=%async_computation.28 | async-start | bytes 4177920 | tf_op jit(solution)/shard_map/psum | solution.py:331
  1691.0 182.8 %reduce-scatter.23.cloned.1.call-start = ((), (), s32[]{:S(2)}) async-start(), calls=%async_computation.27 | async-start | bytes 10027008 | tf_op jit(solution)/shard_map/reduce_scatter | solution.py:99
  1714.7 318.7 %reduce-scatter.15.cloned.1.call-start = ((), (), s32[]{:S(2)}) async-start(), calls=%async_computation.19 | async-start | bytes 10027008 | tf_op jit(solution)/shard_map/reduce_scatter | solution.py:99
  1729.4 144.4 %copy-start.15 = (bf16[512,544]{0,1:T(8,128)(2,1)S(1)}, bf16[512,544]{0,1:T(8,128)(2,1)}, u32[]{:S(2)}) copy-start(bf16[512,544]{0,1:T(8,128)(2,1)} %param.16) | copy-start | bytes 1671172
  1729.4 144.4 %copy-start.45 = (f32[544]{0:T(1024)S(1)}, f32[544]{0:T(1024)}, u32[]{:S(2)}) copy-start(f32[544]{0:T(1024)} %copy-done.44) | copy-start | bytes 6532
  1729.4 144.4 %copy-start.47 = (f32[512,1]{0,1:T(1,128)S(1)}, f32[512,1]{0,1:T(1,128)}, u32[]{:S(2)}) copy-start(f32[512,1]{0,1:T(1,128)} %copy-done.46) | copy-start | bytes 6148
  1729.4 144.4 %copy-start.49 = (f32[512,1]{0,1:T(1,128)S(1)}, f32[512,1]{0,1:T(1,128)}, u32[]{:S(2)}) copy-start(f32[512,1]{0,1:T(1,128)} %copy-done.48) | copy-start | bytes 6148
  1731.9 301.5 %copy-start.8 = (f32[512,544]{0,1:T(8,128)S(1)}, f32[512,544]{0,1:T(8,128)}, u32[]{:S(2)}) copy-start(f32[512,544]{0,1:T(8,128)} %copy-done.7) | copy-start | bytes 3342340
  1731.9 301.5 %copy-start.17 = (f32[512,544]{0,1:T(8,128)S(1)}, f32[512,544]{0,1:T(8,128)}, u32[]{:S(2)}) copy-start(f32[512,544]{0,1:T(8,128)} %reduce-scatter.19.cloned.1.call-done) | copy-start | bytes 3342340
  1742.5 353.2 %copy-start.1 = (bf16[544,544]{1,0:T(8,128)(2,1)S(1)}, bf16[544,544]{1,0:T(8,128)(2,1)}, u32[]{:S(2)}) copy-start(bf16[544,544]{1,0:T(8,128)(2,1)} %param.27) | copy-start | bytes 1775620
  (37 other events, 105.9 us)
Sparse Core Ops, SparseCore 0:
  20.9 79.1 all-gather.8
  122.3 80.8 reduce-scatter.8
  413.6 21.9 all-gather.10
  449.0 155.9 reduce-scatter.10
  607.1 76.2 all-gather.16
  686.0 76.1 all-gather.12
  764.6 104.3 reduce-scatter.16
  871.5 104.8 reduce-scatter.12
  990.2 59.6 all-gather.18
  1058.3 156.0 reduce-scatter.18
  1222.7 77.3 all-gather.20
  1320.1 32.7 reduce-scatter.20
  1370.0 60.2 all-gather.14
  1631.0 46.8 all-gather.22
  1691.1 23.0 all-reduce.6
  1718.1 155.6 reduce-scatter.22
  1877.8 155.6 reduce-scatter.14
where the time goes:
time: 2120 us; the launch traced here: 2100 us
  waiting for transfers between devices  1450 us (68%)
  blocking collectives  176 us (8%)
  matrix products  152 us (7%)
  local copies, waits for them, and re-layouts  128 us (6%)
  other arithmetic  91.1 us (4%)
  starting transfers between devices  91 us (4%)
    reduce_scatter x4, waiting for transfers between devices, product_wide(): lax.psum_scatter(term(jnp.int32(0), lax.axis_size('wide') * share), 'wide...  596 us
    reduce_scatter x4, waiting for transfers between devices, product_narrow(): lax.psum_scatter(term(jnp.int32(0), lax.axis_size('narrow') * share), 'na...  317 us
    all_gather x4, waiting for transfers between devices, rows_wide(): return lax.all_gather(block, 'wide', axis=0, tiled=True)  293 us
    all_gather x4, waiting for transfers between devices, rows_narrow(): return lax.all_gather(block, 'narrow', axis=0, tiled=True)  105 us
    ppermute x16, waiting for transfers between devices, passed_along(): return lax.ppermute(shard, axis, pairs)  95.3 us
    all_to_all x2, blocking collectives, heads_out(): lax.all_to_all(block, 'wide', split_axis=2, concat_axis=0, tiled=True)  91.7 us
    ppermute x16, starting transfers between devices, passed_along(): return lax.ppermute(shard, axis, pairs)  78 us
    psum x1, blocking collectives, shards(): lax.psum((first_gain_part, first_shift_part, merge_bias_part, second_gain...  58.5 us
  transfers between devices with their start and end apart: 35, of which 26 were waited for; matrix products, arithmetic and copies ran while one was open for 10% of the time, Pallas kernels for 0%

commit v1 on v0

v1 whole, which is shorter than its diff:
```python
import functools

import jax
import jax.numpy as jnp
from jax import lax
from jax.experimental import pallas as pl
from jax.experimental.pallas import tpu as pltpu
from jax.sharding import PartitionSpec as P

HEAD = 64
REACH = 4
EPS = 1e-05
NEGATIVE = -1e30
LANES = 128
BF = jnp.bfloat16
F32 = jnp.float32
MESH = pl.DeviceIdType.MESH
ANY = pl.BlockSpec(memory_space=pl.ANY)
DMA = pltpu.SemaphoreType.DMA
SCALE = HEAD ** (-0.5)
LIMIT = 58 * 1024 * 1024


def widths(half):
    main = half // LANES * LANES
    return main, half - main


def rem_rows(rows, half):
    main, rem = widths(half)
    return up16(-(-rows // (main // rem)))


def up16(rows):
    return -(-rows // 16) * 16


def pack(block):
    rows, half = block.shape[-2:]
    main, rem = widths(half)
    count = main // rem
    extra = rem_rows(rows, half)
    lead = block.shape[:-2]
    none = [(0, 0)] * len(lead)
    tail = jnp.pad(block[..., main:], none + [(0, count * extra - rows), (0, 0)])
    tail = jnp.swapaxes(tail.reshape(lead + (count, extra, rem)), -2, -3).reshape(lead + (extra, main))
    return jnp.concatenate([block[..., :main], tail], -2)


def unpack(block, rows, half):
    main, rem = widths(half)
    count = main // rem
    extra = rem_rows(rows, half)
    lead = block.shape[:-2]
    tail = block[..., rows : rows + extra, :].reshape(lead + (extra, count, rem))
    tail = jnp.swapaxes(tail, -2, -3).reshape(lead + (count * extra, rem))[..., :rows, :]
    return block[..., :rows, :], tail


def unpack_half(block, rows, half):
    return jnp.concatenate(unpack(block, rows, half), -1)


def join(blocks, rows, half):
    body, tail = unpack(blocks, rows, half)
    return jnp.concatenate([body[0], body[1], tail[0], tail[1]], -1)


def halves(full):
    half = full.shape[-1] // 2
    main, rem = widths(half)
    edge = 2 * main
    return jnp.stack(
        [
            jnp.concatenate([full[..., :main], full[..., edge : edge + rem]], -1),
            jnp.concatenate([full[..., main:edge], full[..., edge + rem :]], -1),
        ]
    )


def place():
    c, w, n = lax.axis_index("dp"), lax.axis_index("wide"), lax.axis_index("narrow")
    z, y = lax.div(w, 2), lax.rem(w, 2)
    first = (y + c * (1 - 2 * y), n + (1 - c) * (1 - 2 * n))
    second = (y + (1 - c) * (1 - 2 * y), n + c * (1 - 2 * n))
    return c, z, y, n, first, second


def wide_of(z, y):
    return z * 2 + y


def remote(src, dst, send, recv, device):
    return pltpu.make_async_remote_copy(
        src_ref=src, dst_ref=dst, send_sem=send, recv_sem=recv, device_id=device, device_id_type=MESH
    )


def greet(devices):
    barrier = pltpu.get_barrier_semaphore()
    for device in devices:
        pl.semaphore_signal(barrier, inc=1, device_id=device, device_id_type=MESH)
    pl.semaphore_wait(barrier, len(devices))


def partners(outer):
    c, z, y, n, _, _ = place()
    out = [(c, wide_of(lax.rem(z + d, outer), y), n) for d in range(1, outer)]
    out.append((c, wide_of(z, 1 - y), n))
    out.append((c, wide_of(z, y), 1 - n))
    out.append((1 - c, wide_of(z, y), n))
    return out


class Gather:
    def __init__(self, outer, src, out, both, sems):
        self.outer, self.src, self.out, self.both = outer, src, out, both
        self.zs, self.zr, self.fs, self.fr, self.ss, self.sr, self.cs, self.cr, self.local = sems
        self.sent = []

    def block(self, z, y, n):
        c = lax.axis_index("dp")
        return self.out.at[c, wide_of(z, y), n] if self.both else self.out.at[wide_of(z, y), n]

    def go(self, copy):
        copy.start()
        self.sent.append(copy)

    def z_at(self, d):
        return lax.rem(place()[1] + self.outer - d, self.outer)

    def to_first(self, d, src):
        c, z, y, n, first, second = place()
        device = (c, wide_of(z, first[0]), first[1])
        self.go(remote(src, self.block(self.z_at(d), y, n), self.fs.at[d], self.fr.at[d], device))

    def to_second(self, d, src, k):
        c, z, y, n, first, second = place()
        device = (c, wide_of(z, second[0]), second[1])
        dst = self.block(self.z_at(d), y, n) if k == 0 else self.block(self.z_at(d), *first)
        i = k * self.outer + d
        self.go(remote(src, dst, self.ss.at[i], self.sr.at[i], device))

    def to_core(self, i, src, dst):
        if self.both:
            c, z, y, n, _, _ = place()
            self.go(remote(src, dst, self.cs.at[i], self.cr.at[i], (1 - c, wide_of(z, y), n)))

    def start(self):
        c, z, y, n, first, second = place()
        own = self.block(z, y, n)
        self.keep = pltpu.make_async_copy(self.src, own, self.local)
        self.keep.start()
        for d in range(1, self.outer):
            device = (c, wide_of(lax.rem(z + d, self.outer), y), n)
            self.go(remote(self.src, own, self.zs.at[d - 1], self.zr.at[d - 1], device))
        self.to_first(0, self.src)
        self.to_second(0, self.src, 0)
        self.to_core(0, self.src, own)

    def arrived(self, dst, recv):
        c, z, y, n, _, _ = place()
        remote(dst, dst, recv, recv, (1 - c, wide_of(z, y), n)).wait_recv()

    def along_z(self, d):
        c, z, y, n, first, second = place()
        got = self.block(self.z_at(d), y, n)
        self.arrived(got, self.zr.at[d - 1])
        self.to_first(d, got)
        self.to_second(d, got, 0)
        self.to_core(d, got, got)

    def along_first(self, d):
        c, z, y, n, first, second = place()
        got = self.block(self.z_at(d), *first)
        self.arrived(got, self.fr.at[d])
        self.to_second(d, got, 1)
        self.to_core(self.outer + d, got, got)

    def along_second(self, d, k):
        c, z, y, n, first, second = place()
        got = self.block(self.z_at(d), *second) if k == 0 else self.block(self.z_at(d), 1 - y, 1 - n)
        i = k * self.outer + d
        self.arrived(got, self.sr.at[i])
        self.to_core(2 * self.outer + i, got, got)

    def rest(self):
        for d in range(1, self.outer):
            self.along_z(d)
        for d in range(self.outer):
            self.along_first(d)
        for k in range(2):
            for d in range(self.outer):
                self.along_second(d, k)

    def finish(self):
        c, z, y, n, first, second = place()
        if self.both:
            spots = [(y, n), first, second, (1 - y, 1 - n)]
            for k, spot in enumerate(spots):
                for d in range(self.outer):
                    got = self.out.at[1 - c, wide_of(self.z_at(d), spot[0]), spot[1]]
                    self.arrived(got, self.cr.at[k * self.outer + d])
        self.keep.wait()
        for copy in self.sent:
            copy.wait_send()


def gather_sems(outer):
    return [
        DMA((outer,)),
        DMA((outer,)),
        DMA((outer,)),
        DMA((outer,)),
        DMA((2 * outer,)),
        DMA((2 * outer,)),
        DMA((4 * outer,)),
        DMA((4 * outer,)),
        DMA,
    ]


def enter_kernel(outer, xin, cot, sa, sm, x_out, cot_out, ga, gm, xs, xr, hs, hr, ks, kr, ls, *sems):
    c, z, y, n, first, second = place()
    me = wide_of(z, y)
    greet(partners(outer))
    other_n = (c, me, 1 - n)
    other_y = (c, wide_of(z, 1 - y), n)
    other_c = (1 - c, me, n)
    later = (c, wide_of(lax.rem(z + 1, outer), y), n)
    sent = []

    def go(copy):
        copy.start()
        sent.append(copy)

    def arrived(dst, recv):
        remote(dst, dst, recv, recv, other_c).wait_recv()

    def x_send(j):
        src = x_out.at[n, j + 1 - n] if j < 4 else xin.at[1 - n]
        go(remote(src, x_out.at[n, j + 1 - n], hs.at[j], hr.at[j], other_n))

    own = x_out.at[n, pl.ds(4, 2)]
    keep = pltpu.make_async_copy(xin, own, ls.at[0])
    keep.start()
    keep_cot = pltpu.make_async_copy(cot.at[n], cot_out.at[c, n], ls.at[1])
    keep_cot.start()
    go(remote(xin, x_out.at[n, pl.ds(0, 2)], xs.at[0], xr.at[0], later))
    x_send(4)
    heads = Gather(outer, sa, ga, True, sems[:9])
    heads.start()
    arrived(x_out.at[n, pl.ds(0, 2)], xr.at[0])
    keep.wait()
    x_send(0)
    go(
        remote(
            x_out.at[n, pl.ds(4 * (1 - y), 2)],
            x_out.at[n, pl.ds(2, 2)],
            xs.at[1],
            xr.at[1],
            other_y,
        )
    )
    for d in range(1, outer):
        heads.along_z(d)
    arrived(x_out.at[n, pl.ds(2, 2)], xr.at[1])
    for j in (1, 2, 3):
        x_send(j)
    go(remote(cot.at[1 - n], cot_out.at[c, n], ks.at[0], kr.at[0], other_n))
    go(remote(cot.at[n], cot_out.at[c, n], ks.at[1], kr.at[1], other_c))
    for d in range(outer):
        heads.along_first(d)
    mlp = Gather(outer, sm, gm, False, sems[9:])
    mlp.start()
    for k in range(2):
        for d in range(outer):
            heads.along_second(d, k)
    for j in range(5):
        arrived(x_out.at[1 - n, j + n], hr.at[j])
    arrived(cot_out.at[c, 1 - n], kr.at[0])
    go(remote(cot_out.at[c, 1 - n], cot_out.at[c, 1 - n], ks.at[2], kr.at[2], other_c))
    mlp.rest()
    arrived(cot_out.at[1 - c, n], kr.at[1])
    arrived(cot_out.at[1 - c, 1 - n], kr.at[2])
    keep_cot.wait()
    for copy in sent:
        copy.wait_send()
    heads.finish()
    mlp.finish()


def enter(xin, cot, sa, sm):
    wide = lax.axis_size("wide")
    outer = wide // 2
    rows = xin.shape[1:]
    return pl.pallas_call(
        functools.partial(enter_kernel, outer),
        out_shape=(
            jax.ShapeDtypeStruct((2, 6) + rows, BF),
            jax.ShapeDtypeStruct((2, 2) + rows, BF),
            jax.ShapeDtypeStruct((2, wide, 2) + sa.shape, BF),
            jax.ShapeDtypeStruct((wide, 2) + sm.shape, BF),
        ),
        in_specs=[ANY] * 4,
        out_specs=(ANY,) * 4,
        scratch_shapes=[DMA((2,)), DMA((2,)), DMA((5,)), DMA((5,)), DMA((3,)), DMA((3,)), DMA((2,))]
        + gather_sems(outer)
        + gather_sems(outer),
        compiler_params=pltpu.CompilerParams(collective_id=0, has_side_effects=True),
    )(xin, cot, sa, sm)


class Scatter:
    def __init__(self, outer, part, one, two, three, total, fin, sems):
        self.outer, self.part = outer, part
        self.one, self.two, self.three, self.total, self.fin = one, two, three, total, fin
        self.ss, self.sr, self.fs, self.fr, self.zs, self.zr, self.cs, self.cr = sems
        self.sent = []

    def go(self, copy):
        copy.start()
        self.sent.append(copy)

    def arrived(self, dst, recv):
        c, z, y, n, _, _ = place()
        remote(dst, dst, recv, recv, (1 - c, wide_of(z, y), n)).wait_recv()

    def z_at(self, d):
        return lax.rem(place()[1] + d, self.outer)

    def order(self):
        return [d for d in range(1, self.outer)] + [0]

    def start(self):
        c, z, y, n, first, second = place()
        device = (c, wide_of(z, second[0]), second[1])
        for k, spot in ((1, (1 - y, 1 - n)), (0, second)):
            for d in self.order():
                i = k * self.outer + d
                self.go(
                    remote(self.part(self.z_at(d), *spot), self.one.at[i], self.ss.at[i], self.sr.at[i], device)
                )

    def to_first(self, d):
        c, z, y, n, first, second = place()
        device = (c, wide_of(z, first[0]), first[1])
        i = self.outer + d
        self.arrived(self.one.at[i], self.sr.at[i])
        self.one[i] = (self.one[i].astype(F32) + self.part(self.z_at(d), *first)[...].astype(F32)).astype(BF)
        self.go(remote(self.one.at[i], self.two.at[d], self.fs.at[d], self.fr.at[d], device))

    def to_z(self, d):
        c, z, y, n, first, second = place()
        self.arrived(self.one.at[d], self.sr.at[d])
        self.arrived(self.two.at[d], self.fr.at[d])
        value = (
            self.one[d].astype(F32) + self.two[d].astype(F32) + self.part(self.z_at(d), y, n)[...].astype(F32)
        )
        if d == 0:
            self.total[...] = value
        else:
            self.one[d] = value.astype(BF)
            device = (c, wide_of(self.z_at(d), y), n)
            self.go(
                remote(self.one.at[d], self.three.at[d - 1], self.zs.at[d - 1], self.zr.at[d - 1], device)
            )

    def close(self):
        c, z, y, n, first, second = place()
        value = self.total[...]
        for d in range(1, self.outer):
            self.arrived(self.three.at[d - 1], self.zr.at[d - 1])
            value = value + self.three[d - 1].astype(F32)
        self.fin[c] = value
        self.go(remote(self.fin.at[c], self.fin.at[c], self.cs, self.cr, (1 - c, wide_of(z, y), n)))

    def finish(self):
        c = lax.axis_index("dp")
        self.arrived(self.fin.at[1 - c], self.cr)
        for copy in self.sent:
            copy.wait_send()


def scatter_scratch(outer, block):
    return [
        pltpu.VMEM((2 * outer,) + block, BF),
        pltpu.VMEM((outer,) + block, BF),
        pltpu.VMEM((outer,) + block, BF),
        pltpu.VMEM(block, F32),
    ]


def scatter_sems(outer):
    return [
        DMA((2 * outer,)),
        DMA((2 * outer,)),
        DMA((outer,)),
        DMA((outer,)),
        DMA((outer,)),
        DMA((outer,)),
        DMA,
        DMA,
    ]


def leave_kernel(
    outer, pm, pa, pg, lo, mo, ao, xg, lo_out, pcore, acc, got_x, got_z, got_y,
    m1, m2, m3, mt, a1, a2, a3, at, xs, xr, ccs, ccr, *sems
):
    c, z, y, n, first, second = place()
    me = wide_of(z, y)
    greet(partners(outer) + [])
    other_n = (c, me, 1 - n)
    other_y = (c, wide_of(z, 1 - y), n)
    other_c = (1 - c, me, n)
    earlier = (c, wide_of(lax.rem(z + outer - 1, outer), y), n)
    sent = []

    def go(copy):
        copy.start()
        sent.append(copy)

    def arrived(dst, recv):
        remote(dst, dst, recv, recv, other_c).wait_recv()

    mlp = Scatter(outer, lambda z, y, n: pm.at[wide_of(z, y), n], m1, m2, m3, mt, mo, sems[:8])
    heads = Scatter(outer, lambda z, y, n: pcore.at[wide_of(z, y), n], a1, a2, a3, at, ao, sems[8:])
    go(remote(pg.at[1 - n], got_x, xs.at[0], xr.at[0], other_n))
    core_copy = remote(pa.at[1 - c], pcore, ccs, ccr, other_c)
    core_copy.start()
    mlp.start()
    acc[...] = jnp.zeros_like(acc)
    for j in range(5):
        acc[n + j] = pg[n, j].astype(F32)
    arrived(got_x, xr.at[0])
    for j in range(5):
        acc[1 - n + j] = acc[1 - n + j] + got_x[j].astype(F32)
    got_x[pl.ds(0, 2)] = acc[pl.ds(2, 2)].astype(BF)
    go(remote(got_x.at[pl.ds(0, 2)], got_y, xs.at[1], xr.at[1], other_y))
    core_copy.wait_recv()

    @pl.loop(0, 2 * outer)
    def _(i):
        for h in range(2):
            pcore[i, h] = (pcore[i, h].astype(F32) + pa[c, i, h].astype(F32)).astype(BF)

    heads.start()
    arrived(got_y, xr.at[1])
    spot = pl.ds(4 * (1 - y), 2)
    acc[spot] = acc[spot] + got_y[...].astype(F32)
    got_x[pl.ds(2, 2)] = acc[pl.ds(0, 2)].astype(BF)
    go(remote(got_x.at[pl.ds(2, 2)], got_z, xs.at[2], xr.at[2], earlier))
    go(remote(lo.at[1 - n], lo_out.at[n], xs.at[3], xr.at[3], other_n))
    lo_out[n] = lo[n]
    for d in mlp.order():
        mlp.to_first(d)
    for d in mlp.order():
        mlp.to_z(d)
    for d in heads.order():
        heads.to_first(d)
    for d in heads.order():
        heads.to_z(d)
    mlp.close()
    arrived(got_z, xr.at[2])
    xg[...] = (acc[pl.ds(4, 2)] + got_z[...].astype(F32)).astype(BF)
    heads.close()
    arrived(lo_out.at[1 - n], xr.at[3])
    core_copy.wait_send()
    for copy in sent:
        copy.wait_send()
    mlp.finish()
    heads.finish()


def leave(pm, pa, pg, lo):
    wide = lax.axis_size("wide")
    outer = wide // 2
    bm, ba, bx = pm.shape[2:], pa.shape[3:], lo.shape[1:]
    vmem = pl.BlockSpec(memory_space=pltpu.VMEM)
    return pl.pallas_call(
        functools.partial(leave_kernel, outer),
        out_shape=(
            jax.ShapeDtypeStruct((2,) + bm, F32),
            jax.ShapeDtypeStruct((2,) + ba, F32),
            jax.ShapeDtypeStruct((2,) + bx, BF),
            jax.ShapeDtypeStruct((2,) + bx, BF),
        ),
        in_specs=[vmem] * 4,
        out_specs=(vmem,) * 4,
        scratch_shapes=[
            pltpu.VMEM(pa.shape[1:], BF),
            pltpu.VMEM((6,) + bx, F32),
            pltpu.VMEM((5,) + bx, BF),
            pltpu.VMEM((2,) + bx, BF),
            pltpu.VMEM((2,) + bx, BF),
        ]
        + scatter_scratch(outer, bm)
        + scatter_scratch(outer, ba)
        + [DMA((4,)), DMA((4,)), DMA, DMA]
        + scatter_sems(outer)
        + scatter_sems(outer),
        compiler_params=pltpu.CompilerParams(
            collective_id=1, has_side_effects=True, vmem_limit_bytes=LIMIT
        ),
    )(pm, pa, pg, lo)


def dot(left, right, dims):
    return lax.dot_general(left, right, ((dims[0], dims[1]), ((), ())), preferred_element_type=F32)


NN = ((1,), (0,))
NT = ((1,), (1,))
TN = ((0,), (0,))


def spread(tail, rows, rem):
    extra = tail.shape[0]
    count = -(-rows // extra)
    return jnp.concatenate([tail[:, k * rem : (k + 1) * rem] for k in range(count)], 0)[:rows]


def squeezed(block, extra, main):
    rows, rem = block.shape
    count = -(-rows // extra)
    short = count * extra - rows
    if short:
        block = jnp.concatenate([block, jnp.zeros((short, rem), block.dtype)], 0)
    parts = [block[k * extra : (k + 1) * extra] for k in range(count)]
    if count * rem < main:
        parts.append(jnp.zeros((extra, main - count * rem), block.dtype))
    return jnp.concatenate(parts, 1)


def store_packed(ref, index, value, main, rem):
    rows = value.shape[0]
    for h in range(2):
        at = ref.at[(h,) + index]
        at[0:rows, :] = value[:, h * main : (h + 1) * main].astype(ref.dtype)
        low = value[:, 2 * main + h * rem : 2 * main + (h + 1) * rem]
        at[rows:, :] = squeezed(low, at.shape[0] - rows, main).astype(ref.dtype)


def gelu_and_slope(u):
    share = 0.5 * (1.0 + lax.erf(u * 0.7071067811865476))
    return u * share, share + u * (jnp.exp(-0.5 * u * u) * 0.3989422804014327)


def mlp_kernel(
    wide, fc, rem, low2, cot_in, gm, residual, normed2, scale2, gain2, bias_u, bias_d,
    pm, lo, grad_res, sums, up_sum,
    weights, grads, tails, cot, low2_all, acc, got, wsem, tsem, psem, qsem, xs, xr
):
    c, w, n = lax.axis_index("dp"), lax.axis_index("wide"), lax.axis_index("narrow")
    other = (1 - c, w, n)
    rows, width = low2.shape
    main = gm.shape[3]
    extra = gm.shape[2] - 2 * fc
    nf = wide * fc
    greet([other])
    mine, theirs = pl.ds(c * rows, rows), pl.ds((1 - c) * rows, rows)
    swap_low = remote(low2, low2_all.at[mine], xs.at[0], xr.at[0], other)
    swap_low.start()

    def weight_copies(i):
        out = []
        for h in range(2):
            for k in range(2):
                out.append(
                    pltpu.make_async_copy(
                        gm.at[i, h, pl.ds(k * fc, fc)],
                        weights.at[k, pl.ds(i * fc, fc), pl.ds(h * main, main)],
                        wsem.at[i, h, k],
                    )
                )
            out.append(pltpu.make_async_copy(gm.at[i, h, pl.ds(2 * fc, extra)], tails.at[i, h], tsem.at[i, h]))
        return out

    @pl.loop(0, wide)
    def _(i):
        for copy in weight_copies(i):
            copy.start()

    low2_all[mine] = low2[...]
    for k in range(2):
        span = slice(k * rows, (k + 1) * rows)
        for h in range(2):
            cot[span, h * main : (h + 1) * main] = cot_in[k, h, 0:rows, :]
        cot[span, 2 * main :] = jnp.concatenate(
            [spread(cot_in[k, h, rows:, :].astype(F32), rows, rem) for h in range(2)], 1
        ).astype(BF)

    @pl.loop(0, wide)
    def _(i):
        for copy in weight_copies(i):
            copy.wait()
        both = jnp.concatenate([spread(tails[i, h].astype(F32), 2 * fc, rem) for h in range(2)], 1).astype(BF)
        for k in range(2):
            weights[k, pl.ds(i * fc, fc), 2 * main :] = both[k * fc : (k + 1) * fc]

    acc[...] = jnp.zeros_like(acc)
    swap_low.wait_recv()

    def step(start, size):
        at = pl.ds(start, size)
        before = dot(low2_all[...], weights[0, at, :], NT) + bias_u[:, at]
        hidden, slope = gelu_and_slope(before)
        hidden = hidden.astype(BF)
        acc[0] += dot(hidden, weights[1, at, :], NN)
        grads[1, at, :] = dot(hidden, cot[...], TN).astype(BF)
        grad = dot(cot[...], weights[1, at, :], NT) * slope
        grad = grad.astype(BF)
        up_sum[:, at] = jnp.sum(grad.astype(F32), 0, keepdims=True)
        acc[1] += dot(grad, weights[0, at, :], NN)
        grads[0, at, :] = dot(grad, low2_all[...], TN).astype(BF)

    size = 256
    full = nf // size

    @pl.loop(0, full)
    def _(j):
        step(pl.multiple_of(j * size, size), size)

    if nf % size:
        step(full * size, nf % size)

    swap_acc = remote(acc.at[:, theirs], got, xs.at[1], xr.at[1], other)
    swap_acc.start()

    def grad_copies(i):
        out = []
        for h in range(2):
            for k in range(2):
                out.append(
                    pltpu.make_async_copy(
                        grads.at[k, pl.ds(i * fc, fc), pl.ds(h * main, main)],
                        pm.at[i, h, pl.ds(k * fc, fc)],
                        psem.at[i, h, k],
                    )
                )
        return out

    def tail_copies(i):
        return [
            pltpu.make_async_copy(tails.at[i, h], pm.at[i, h, pl.ds(2 * fc, extra)], qsem.at[i, h])
            for h in range(2)
        ]

    @pl.loop(0, wide)
    def _(i):
        for copy in grad_copies(i):
            copy.start()
        low = jnp.concatenate([grads[k, pl.ds(i * fc, fc), 2 * main :] for k in range(2)], 0).astype(F32)
        for h in range(2):
            tails[i, h] = squeezed(low[:, h * rem : (h + 1) * rem], extra, main).astype(BF)
        for copy in tail_copies(i):
            copy.start()

    swap_acc.wait_recv()
    result = residual[...] + (acc[0, mine] + got[0]) + bias_d[...]
    store_packed(lo, (), result, main, rem)
    grad_low2 = acc[1, mine] + got[1]
    scaled = grad_low2 * gain2[...]
    first = jnp.mean(scaled, 1, keepdims=True)
    second = jnp.mean(scaled * normed2[...], 1, keepdims=True)
    grad_out = cot[mine].astype(F32)
    total = grad_out + scale2[...] * (scaled - first - normed2[...] * second)
    grad_res[...] = total
    sums[0:1] = jnp.sum(grad_low2 * normed2[...], 0, keepdims=True)
    sums[1:2] = jnp.sum(grad_low2, 0, keepdims=True)
    sums[2:3] = jnp.sum(total.astype(BF).astype(F32), 0, keepdims=True)
    sums[3:4] = jnp.sum(grad_out, 0, keepdims=True)
    sums[4:8] = jnp.zeros((4, width), F32)

    @pl.loop(0, wide)
    def _(i):
        for copy in grad_copies(i) + tail_copies(i):
            copy.wait()

    swap_low.wait_send()
    swap_acc.wait_send()


def mlp(low2, cot_in, gm, residual, normed2, scale2, gain2, bias_u, bias_d, rem):
    wide = gm.shape[0]
    rows, width = low2.shape
    nf = bias_u.shape[1]
    fc = nf // wide
    main = gm.shape[3]
    extra = gm.shape[2] - 2 * fc
    vmem = pl.BlockSpec(memory_space=pltpu.VMEM)
    return pl.pallas_call(
        functools.partial(mlp_kernel, wide, fc, rem),
        out_shape=(
            jax.ShapeDtypeStruct(gm.shape, BF),
            jax.ShapeDtypeStruct((2,) + cot_in.shape[2:], BF),
            jax.ShapeDtypeStruct((rows, width), F32),
            jax.ShapeDtypeStruct((8, width), F32),
            jax.ShapeDtypeStruct((1, nf), F32),
        ),
        in_specs=[vmem, vmem, ANY] + [vmem] * 6,
        out_specs=(ANY, vmem, vmem, vmem, vmem),
        scratch_shapes=[
            pltpu.VMEM((2, nf, width), BF),
            pltpu.VMEM((2, nf, width), BF),
            pltpu.VMEM((wide, 2, extra, main), BF),
            pltpu.VMEM((2 * rows, width), BF),
            pltpu.VMEM((2 * rows, width), BF),
            pltpu.VMEM((2, 2 * rows, width), F32),
            pltpu.VMEM((2, rows, width), F32),
            DMA((wide, 2, 2)),
            DMA((wide, 2)),
            DMA((wide, 2, 2)),
            DMA((wide, 2)),
            DMA((2,)),
            DMA((2,)),
        ],
        compiler_params=pltpu.CompilerParams(
            collective_id=2, has_side_effects=True, vmem_limit_bytes=LIMIT
        ),
    )(low2, cot_in, gm, residual, normed2, scale2, gain2, bias_u, bias_d)


def fill_mask(q_seg, k_seg, mask):
    keys, queries = mask.shape
    key = lax.broadcasted_iota(jnp.int32, (keys, queries), 0)
    query = lax.broadcasted_iota(jnp.int32, (keys, queries), 1) + (keys - queries)
    allowed = (k_seg[...] == q_seg[...]) & (key <= query)
    mask[...] = jnp.where(allowed, 0.0, NEGATIVE)


def turned(block):
    return block.astype(F32).T


def attend_kernel(q, k, v, q_seg, k_seg, out, lse, mask):
    @pl.when(pl.program_id(0) == 0)
    def _():
        fill_mask(q_seg, k_seg, mask)

    q_t = turned(q[...]) * SCALE
    row = lax.broadcasted_iota(jnp.int32, q_t.shape, 0)
    parts = []
    lse[...] = jnp.zeros_like(lse)
    for h in range(2):
        mine = (row >= h * HEAD) & (row < (h + 1) * HEAD)
        q_h = jnp.where(mine, q_t, 0.0).astype(BF)
        s = dot(k[...], q_h, NN) + mask[...]
        top = jnp.max(s, 0, keepdims=True)
        p = jnp.exp(s - top)
        total = jnp.sum(p, 0, keepdims=True)
        p = (p * (1.0 / total)).astype(BF)
        parts.append(dot(v[...], p, TN)[h * HEAD : (h + 1) * HEAD])
        lse[0, pl.ds(h, 1), :] = top + jnp.log(total)
    out[...] = jnp.concatenate(parts, 0).T.astype(BF)


def attend(q, k, v, q_seg, k_seg):
    queries, width = q.shape
    keys = k.shape[0]
    pairs = width // LANES
    return pl.pallas_call(
        attend_kernel,
        grid=(pairs,),
        out_shape=(
            jax.ShapeDtypeStruct((queries, width), BF),
            jax.ShapeDtypeStruct((pairs, 8, queries), F32),
        ),
        in_specs=[
            pl.BlockSpec((queries, LANES), lambda i: (0, i)),
            pl.BlockSpec((keys, LANES), lambda i: (0, i)),
            pl.BlockSpec((keys, LANES), lambda i: (0, i)),
            pl.BlockSpec((1, queries), lambda i: (0, 0)),
            pl.BlockSpec((keys, 1), lambda i: (0, 0)),
        ],
        out_specs=(
            pl.BlockSpec((queries, LANES), lambda i: (0, i)),
            pl.BlockSpec((1, 8, queries), lambda i: (i, 0, 0)),
        ),
        scratch_shapes=[pltpu.VMEM((keys, queries), F32)],
        compiler_params=pltpu.CompilerParams(vmem_limit_bytes=LIMIT),
    )(q, k, v, q_seg, k_seg)


def attend_back_kernel(q, k, v, g, lse, q_seg, k_seg, dq, dk, dv, mask):
    @pl.when(pl.program_id(0) == 0)
    def _():
        fill_mask(q_seg, k_seg, mask)

    q_n = q[...].astype(F32) * SCALE
    g_n = g[...].astype(F32)
    q_t, g_t = q_n.T, g_n.T
    row = lax.broadcasted_iota(jnp.int32, q_t.shape, 0)
    lane = lax.broadcasted_iota(jnp.int32, q_n.shape, 1)
    parts = []
    dk_sum = dv_sum = None
    for h in range(2):
        in_row = (row >= h * HEAD) & (row < (h + 1) * HEAD)
        in_lane = (lane >= h * HEAD) & (lane < (h + 1) * HEAD)
        s = dot(k[...], jnp.where(in_row, q_t, 0.0).astype(BF), NN) + mask[...]
        p = jnp.exp(s - lse[0, pl.ds(h, 1), :])
        dp = dot(v[...], jnp.where(in_row, g_t, 0.0).astype(BF), NN)
        delta = jnp.sum(p * dp, 0, keepdims=True)
        ds = (p * (dp - delta)).astype(BF)
        one = dot(ds, jnp.where(in_lane, q_n, 0.0).astype(BF), NN)
        two = dot(p.astype(BF), jnp.where(in_lane, g_n, 0.0).astype(BF), NN)
        dk_sum = one if dk_sum is None else dk_sum + one
        dv_sum = two if dv_sum is None else dv_sum + two
        parts.append(dot(k[...], ds, TN)[h * HEAD : (h + 1) * HEAD] * SCALE)
    dq[...] = jnp.concatenate(parts, 0).T.astype(BF)
    dk[...] = dk_sum.astype(BF)
    dv[...] = dv_sum.astype(BF)


def attend_back(q, k, v, g, lse, q_seg, k_seg):
    queries, width = q.shape
    keys = k.shape[0]
    pairs = width // LANES
    few = pl.BlockSpec((queries, LANES), lambda i: (0, i))
    many = pl.BlockSpec((keys, LANES), lambda i: (0, i))
    return pl.pallas_call(
        attend_back_kernel,
        grid=(pairs,),
        out_shape=(
            jax.ShapeDtypeStruct((queries, width), BF),
            jax.ShapeDtypeStruct((keys, width), BF),
            jax.ShapeDtypeStruct((keys, width), BF),
        ),
        in_specs=[
            few,
            many,
            many,
            few,
            pl.BlockSpec((1, 8, queries), lambda i: (i, 0, 0)),
            pl.BlockSpec((1, queries), lambda i: (0, 0)),
            pl.BlockSpec((keys, 1), lambda i: (0, 0)),
        ],
        out_specs=(few, many, many),
        scratch_shapes=[pltpu.VMEM((keys, queries), F32)],
        compiler_params=pltpu.CompilerParams(vmem_limit_bytes=LIMIT),
    )(q, k, v, g, lse, q_seg, k_seg)


def norm_forward(values, gain, shift):
    mean = jnp.mean(values, 1, keepdims=True)
    centred = values - mean
    scale = lax.rsqrt(jnp.mean(centred * centred, 1, keepdims=True) + EPS)
    normed = centred * scale
    return normed, scale, (normed * gain + shift).astype(BF)


def norm_backward(grad, normed, scale, gain):
    scaled = grad * gain
    first = jnp.mean(scaled, 1, keepdims=True)
    second = jnp.mean(scaled * normed, 1, keepdims=True)
    back = scale * (scaled - first - normed * second)
    return back, jnp.sum(grad * normed, 0), jnp.sum(grad, 0)


def shards(
    layer_input,
    doc_segments,
    first_gain,
    first_shift,
    heads_weight,
    query_bias,
    value_bias,
    merge_weight,
    merge_bias,
    second_gain,
    second_shift,
    up_weight,
    up_bias,
    down_weight,
    down_bias,
    out_cotangent,
):
    parts = lax.axis_size("narrow")
    wide = lax.axis_size("wide")
    c, w, n = lax.axis_index("dp"), lax.axis_index("wide"), lax.axis_index("narrow")
    half = heads_weight.shape[0]
    width = half * parts
    padded = -(-width // LANES) * LANES
    cols = heads_weight.shape[2]
    units = up_weight.shape[1]
    hc, fc = cols // 2, up16(units // 2)
    short = fc - units // 2
    rows = layer_input.shape[0] // parts
    span = (REACH + 1) * rows

    by_half = heads_weight.transpose(1, 2, 0).reshape(3, 2, hc, half)
    heads_rows = lax.dynamic_index_in_dim(by_half, c, 1, False).reshape(3 * hc, half)
    merge_rows = lax.dynamic_slice_in_dim(merge_weight, c * hc, hc, 0)
    up_rows = lax.dynamic_slice_in_dim(up_weight, c * (units // 2), units // 2, 1).T
    down_rows = lax.dynamic_slice_in_dim(down_weight, c * (units // 2), units // 2, 0)
    up_rows = jnp.pad(up_rows, ((0, short), (0, 0)))
    down_rows = jnp.pad(down_rows, ((0, short), (0, 0)))
    line = lambda *v: jnp.pad(jnp.concatenate(v), (0, half - sum(e.shape[0] for e in v)))
    vectors = jnp.stack(
        [
            first_gain,
            first_shift,
            merge_bias,
            second_gain,
            second_shift,
            down_bias,
            line(query_bias, value_bias),
            line(up_bias),
        ]
    )
    vectors = jnp.pad(vectors, ((0, up16(4 * hc + 8) - 4 * hc - 8), (0, 0)))
    sa = jnp.concatenate([heads_rows, merge_rows, vectors], 0)
    rows_a = sa.shape[0]
    sm = jnp.concatenate([up_rows, down_rows], 0)
    xin = pack(layer_input.reshape(2, rows, half))
    cot_in = pack(out_cotangent.reshape(2, rows, half))

    x_all, cot_all, ga, gm = enter(xin, cot_in, pack(sa), pack(sm))

    x_all = lax.dynamic_slice_in_dim(x_all, n, REACH + 1, 1)
    x = join(x_all, rows, half).reshape(span, width).astype(F32)
    full_a = join(jnp.moveaxis(ga, 2, 0), rows_a, half)
    weight = full_a[:, :, : 3 * hc].reshape(2, wide, 3, hc, width).transpose(2, 1, 0, 3, 4)
    weight = jnp.pad(weight.reshape(3, width, width), ((0, 0), (0, padded - width), (0, 0)))
    merge = full_a[:, :, 3 * hc : 4 * hc].transpose(1, 0, 2, 3).reshape(width, width)
    merge = jnp.pad(merge, ((0, padded - width), (0, 0)))
    gain1, shift1, bias_m, gain2, shift2, bias_d = full_a[0, 0, 4 * hc : 4 * hc + 6].astype(F32)
    wide_rows = unpack_half(ga[0, :, 0], rows_a, half)[:, 4 * hc + 6 : 4 * hc + 8].astype(F32)
    bias_q = jnp.pad(wide_rows[:, 0, :cols].reshape(width), (0, padded - width))
    bias_v = jnp.pad(wide_rows[:, 0, cols : 2 * cols].reshape(width), (0, padded - width))
    bias_u = lax.dynamic_slice_in_dim(wide_rows[:, 1], c * (units // 2), units // 2, 1)
    bias_u = jnp.pad(bias_u, ((0, 0), (0, short))).reshape(1, wide * fc)
    x, weight, merge = lax.optimization_barrier((x, weight, merge))

    normed1, scale1, low1 = norm_forward(x, gain1, shift1)
    own = low1[span - rows :]
    query = (dot(own, weight[0], NT) + bias_q).astype(BF)
    key = dot(low1, weight[1], NT).astype(BF)
    value = (dot(low1, weight[2], NT) + bias_v).astype(BF)
    seg_row = lax.dynamic_index_in_dim(doc_segments, c, 0, keepdims=False)
    start = (w * parts + n) * rows
    key_pos = start - REACH * rows + jnp.arange(span, dtype=jnp.int32)
    ahead = jnp.concatenate([jnp.full((REACH * rows,), -1, jnp.int32), seg_row])
    k_seg = lax.dynamic_slice_in_dim(ahead, start, span, 0)[:, None]
    q_seg = lax.dynamic_slice_in_dim(seg_row, start, rows, 0)[None]
    mixed, lse = attend(query, key, value, q_seg, k_seg)
    residual = x[span - rows :] + dot(mixed, merge, NN) + bias_m
    normed2, scale2, low2 = norm_forward(residual, gain2, shift2)

    pm, lo, grad_residual, sums2, up_sum = mlp(
        low2, cot_all, gm, residual, normed2, scale2, gain2[None], bias_u, bias_d[None], half - widths(half)[0]
    )
    up_bias_grad = up_sum.reshape(wide, fc)[:, : units // 2]
    grad_branch = grad_residual.astype(BF)
    merge_grad = dot(mixed, grad_branch, TN)[:width]
    grad_mixed = dot(grad_branch, merge, NT).astype(BF)
    dq, dk, dv = attend_back(query, key, value, grad_mixed, lse, q_seg, k_seg)
    grad_low1 = dot(dk, weight[1], NN) + dot(dv, weight[2], NN)
    grad_low1 = grad_low1.at[span - rows :].add(dot(dq, weight[0], NN))
    back1, gain1_grad, shift1_grad = norm_backward(grad_low1, normed1, scale1, gain1)
    back1 = back1.at[span - rows :].add(grad_residual)
    heads_grad = jnp.stack(
        [dot(dq, own, TN)[:width], dot(dk, low1, TN)[:width], dot(dv, low1, TN)[:width]]
    )
    pa = jnp.concatenate(
        [
            heads_grad.reshape(3, wide, 2, hc, width).transpose(2, 1, 0, 3, 4).reshape(2, wide, 3 * hc, width),
            merge_grad.reshape(wide, 2, hc, width).transpose(1, 0, 2, 3),
        ],
        2,
    ).astype(BF)
    pa = jnp.pad(pa, ((0, 0), (0, 0), (0, up16(4 * hc) - 4 * hc), (0, 0)))
    pa = jnp.moveaxis(pack(halves(pa)), 0, 2)
    pg = pack(halves(back1.reshape(REACH + 1, rows, width).astype(BF)))

    mo, ao, xg, lo_out = leave(pm, pa, pg, lo)

    layer_output = unpack_half(lo_out, rows, half).reshape(2 * rows, half)
    input_grad = unpack_half(xg, rows, half).reshape(2 * rows, half)
    ao = unpack_half(ao, up16(4 * hc), half)
    heads_total = ao[:, : 3 * hc].reshape(2, 3, hc, half).transpose(3, 1, 0, 2).reshape(half, 3, cols)
    merge_total = ao[:, 3 * hc : 4 * hc].reshape(cols, half)
    mo = unpack_half(mo, 2 * fc, half)
    up_total = mo[:, : units // 2].reshape(units, half).T
    down_total = mo[:, fc : fc + units // 2].reshape(units, half)

    lines = jnp.stack(
        [
            gain1_grad,
            shift1_grad,
            sums2[2],
            sums2[0],
            sums2[1],
            sums2[3],
        ]
    )
    up_lines = jnp.where(jnp.arange(2)[:, None, None] == c, up_bias_grad[None], 0.0)
    lines, q_sum, v_sum, up_lines = lax.psum(
        (lines, jnp.sum(dq, 0, dtype=F32)[:width], jnp.sum(dv, 0, dtype=F32)[:width], up_lines),
        ("dp", "wide", "narrow"),
    )
    lines = lax.dynamic_index_in_dim(halves(lines), n, 0, False)
    query_total = lax.dynamic_slice_in_dim(q_sum, w * cols, cols, 0)
    value_total = lax.dynamic_slice_in_dim(v_sum, w * cols, cols, 0)
    up_bias_total = lax.dynamic_index_in_dim(up_lines, w, 1, False).reshape(units)
    return (
        layer_output,
        input_grad,
        lines[0],
        lines[1],
        heads_total,
        query_total,
        value_total,
        merge_total,
        lines[2],
        lines[3],
        lines[4],
        up_total,
        up_bias_total,
        down_total,
        lines[5],
    )


def solution(mesh):
    return jax.shard_map(
        shards,
        mesh=mesh,
        in_specs=(
            P(("dp", "wide"), "narrow"),
            P(),
            P("narrow"),
            P("narrow"),
            P("narrow", None, "wide"),
            P("wide"),
            P("wide"),
            P("wide", "narrow"),
            P("narrow"),
            P("narrow"),
            P("narrow"),
            P("narrow", "wide"),
            P("wide"),
            P("wide", "narrow"),
            P("narrow"),
            P(("dp", "wide"), "narrow"),
        ),
        out_specs=(
            P(("dp", "wide"), "narrow"),
            P(("dp", "wide"), "narrow"),
            P("narrow"),
            P("narrow"),
            P("narrow", None, "wide"),
            P("wide"),
            P("wide"),
            P("wide", "narrow"),
            P("narrow"),
            P("narrow"),
            P("narrow"),
            P("narrow", "wide"),
            P("wide"),
            P("wide", "narrow"),
            P("narrow"),
        ),
        check_vma=False,
    )
```

time: 2120 us -> 814 us (0.38)
  waiting for transfers between devices: 1450 us -> 0 us
  Pallas kernels: 0 us -> 443 us
  blocking collectives: 176 us -> 48 us
  matrix products: 152 us -> 51 us
  starting transfers between devices: 91 us -> 0 us
  local copies, waits for them, and re-layouts: 128 us -> 187 us
    reduce_scatter x8 -> x0, waiting for transfers between devices: 913 us -> none  [the longest x4 596 us: product_wide(): lax.psum_scatter(term(jnp.int32(0), lax.axis_size('wide') * share), 'wide...]
    pallas_call x0 -> x5, Pallas kernels: none -> 443 us  [the longest x1 179 us: leave(): pl.pallas_call(functools.partial(leave_kernel, outer), out_shape=(jax.Sha...]
    all_gather x8 -> x0, waiting for transfers between devices: 399 us -> none  [the longest x4 293 us: rows_wide(): return lax.all_gather(block, 'wide', axis=0, tiled=True)]
    dot_general x42 -> x12, matrix products: 152 us -> 51 us  [dot(): lax.dot_general(left, right, ((dims[0], dims[1]), ((), ())), preferred_el...]
    ppermute x16 -> x0, waiting for transfers between devices: 95.3 us -> none  [passed_along(): return lax.ppermute(shard, axis, pairs)]
    all_to_all x2 -> x0, blocking collectives: 91.7 us -> none  [heads_out(): lax.all_to_all(block, 'wide', split_axis=2, concat_axis=0, tiled=True)]
    ppermute x16 -> x0, starting transfers between devices: 78 us -> none  [passed_along(): return lax.ppermute(shard, axis, pairs)]
    convert_element_type x21 -> x5, other arithmetic: 59.7 us -> 12.9 us  [the longest x2 5.43 us: norm_forward(): return (normed, scale, (normed * gain + shift).astype(BF))]
  transfers between devices with their start and end apart: 35 -> 0, of which waited for: 26 -> 0; matrix products, arithmetic and copies ran while one was open for 10% -> 0% of each run, Pallas kernels for 0% -> 0%
where the time goes in v1:
time: 814 us; the launch traced here: 806 us
  Pallas kernels  443 us (54%)
  local copies, waits for them, and re-layouts  187 us (23%)
  other arithmetic  74.8 us (9%)
  matrix products  51 us (6%)
  blocking collectives  48 us (6%)
    pallas_call x1, Pallas kernels, leave(): pl.pallas_call(functools.partial(leave_kernel, outer), out_shape=(jax.Sha...  179 us
    pallas_call x1, Pallas kernels, enter(): pl.pallas_call(functools.partial(enter_kernel, outer), out_shape=(jax.Sha...  169 us
    dot_general x12, matrix products, dot(): lax.dot_general(left, right, ((dims[0], dims[1]), ((), ())), preferred_el...  51 us
    psum x1, blocking collectives, shards(): lax.psum((lines, jnp.sum(dq, 0, dtype=F32)[:width], jnp.sum(dv, 0, dtype=...  48 us
    pallas_call x1, Pallas kernels, mlp(): pl.pallas_call(functools.partial(mlp_kernel, wide, fc, rem), out_shape=(j...  46.1 us
    pallas_call x1, Pallas kernels, attend_back(): pl.pallas_call(attend_back_kernel, grid=(pairs,), out_shape=(jax.ShapeDty...  25.9 us
    pallas_call x1, Pallas kernels, attend(): pl.pallas_call(attend_kernel, grid=(pairs,), out_shape=(jax.ShapeDtypeStr...  22.9 us
    concatenate x2, local copies, waits for them, and re-layouts, join(): return jnp.concatenate([body[0], body[1], tail[0], tail[1]], -1)  22 us

profile of v1, /device:TPU:11, one launch (start us, length us, event | category | flops | bytes accessed | tf_op | source)
XLA Modules:
  0.0 805.8 jit_solution(12808229766433460500)
XLA Ops:
  16.8 169.1 %shard_map.271 = (bf16[2,6,272,512]{3,2,1,0:T(8,128)(2,1)}, bf16[2,2,272,512]{3,2,1,0:T(8,128)(2,1)}, bf16[2,8,2,320,512]{4,3,2,1,0:T(8,128)(2,1)}, bf16[8,2,592,512]{3,2,1,0:T(8,128)(2,1)}) custom-call(bf16[2,272,512]{2,1,0:T(8,128)(2,1)} %get-tuple-element.135.xin, bf16[2,272,512]{2,1,0:T(8,128)(2,1)} %get-tuple-element.136.cot, ...), custom_call_target="tpu_custom_call" | custom-call | tf_op jit(solution)/shard_map/pallas_call | solution.py:297
  186.9 2.0 constant_dynamic-slice_fusion
  192.3 5.5 concatenate.109
  197.8 2.3 slice.400
  200.1 1.9 slice_bitcast_fusion.3
  206.5 4.8 convert_element_type.61
  211.3 3.7 reshape.330
  215.1 3.3 copy.108
  218.5 8.3 %slice_bitcast_fusion = (bf16[2,8,288,512]{3,2,1,0:T(8,128)(2,1)}, bf16[2,8,288,512]{3,2,1,0:T(8,128)(2,1)}) fusion(bf16[2,2,8,320,512]{4,3,0,2,1:T(8,128)(2,1)} %bitcast.168), kind=kLoop, calls=%fused_computation.37 | loop fusion | bytes 18874368 | tf_op jit(solution)/shard_map/squeeze | solution.py:66
  226.8 16.5 %concatenate.110 = bf16[2,8,288,1088]{3,2,1,0:T(8,128)(2,1)} concatenate(bf16[2,8,288,512]{3,2,1,0:T(8,128)(2,1)} %get-tuple-element.105, bf16[2,8,288,512]{3,2,1,0:T(8,128)(2,1)} %get-tuple-element.104, bf16[2,8,288,32]{3,2,1,0:T(8,128)(2,1)S(1)} %get-tuple-element.109, bf16[2,8,288,32]{3,2,1,0:T(8,128)(2,1)S(1)} %get-tuple-element.108), dimensions={3} | concatenate | bytes 20054016 | tf_op jit(solution)/shard_map/concatenate | solution.py:66
  244.7 4.3 slice_bitcast_fusion.2
  249.0 3.2 slice-done.4
  252.1 4.6 copy.109
  256.7 2.0 copy.111
  258.7 2.5 reshape.334
  261.1 3.4 pad.45
  264.6 7.2 copy.110
  271.8 11.1 %reshape.333 = bf16[3,1088,1088]{2,1,0:T(8,128)(2,1)} reshape(bf16[3,8,2,68,1088]{4,3,2,1,0:T(8,128)(2,1)} %copy.110) | data formatting | bytes 14204928 | tf_op jit(solution)/shard_map/reshape | solution.py:925
  282.9 6.9 pad.44
  289.8 3.0 reduce_sum.90
  292.8 3.6 multiply_reduce_fusion.2
  296.4 3.9 add_convert_fusion
  300.4 1.9 fusion.22.q
  302.3 5.8 fusion.5.v
  308.0 5.8 convolution_convert_fusion.k
  313.8 22.9 %shard_map.272 = (bf16[256,1152]{1,0:T(8,128)(2,1)}, f32[9,8,256]{2,1,0:T(8,128)}) custom-call(bf16[256,1152]{1,0:T(8,128)(2,1)} %fusion.22.q, bf16[1280,1152]{1,0:T(8,128)(2,1)} %convolution_convert_fusion.k, bf16[1280,1152]{1,0:T(8,128)(2,1)} %fusion.5.v, s32[1,256]{1,0:T(1,128)} %dynamic_slice.48.q_seg, s32[1280,1]{1,0:T(8,128)} %broadcast_in_dim.41.k_seg), custom_call_target="tpu_custom_call" | custom-call | tf_op jit(solution)/shard_map/pallas_call | solution.py:763
  336.7 2.6 fusion.59
  341.9 46.1 %shard_map.273 = (bf16[8,2,592,512]{3,2,1,0:T(8,128)(2,1)}, bf16[2,272,512]{2,1,0:T(8,128)(2,1)}, f32[256,1088]{1,0:T(8,128)}, f32[8,1088]{1,0:T(8,128)}, f32[1,2176]{1,0:T(1,128)}) custom-call(bf16[256,1088]{1,0:T(8,128)(2,1)} %get-tuple-element.102.low2, bf16[2,2,272,512]{3,2,1,0:T(8,128)(2,1)} %get-tuple-element.66.cot_in, ...), custom_call_target="tpu_custom_call" | custom-call | tf_op jit(solution)/shard_map/pallas_call | solution.py:693
  388.0 3.2 convolution_convert_fusion.1.g
  391.2 25.9 %shard_map.274 = (bf16[256,1152]{1,0:T(8,128)(2,1)}, bf16[1280,1152]{1,0:T(8,128)(2,1)}, bf16[1280,1152]{1,0:T(8,128)(2,1)}) custom-call(bf16[256,1152]{1,0:T(8,128)(2,1)} %fusion.22.q, bf16[1280,1152]{1,0:T(8,128)(2,1)} %convolution_convert_fusion.k, bf16[1280,1152]{1,0:T(8,128)(2,1)} %fusion.5.v, bf16[256,1152]{1,0:T(8,128)(2,1)} %convolution_convert_fusion.1.g, ...), custom_call_target="tpu_custom_call" | custom-call | tf_op jit(solution)/shard_map/pallas_call | solution.py:822
  418.5 2.3 convert_reduce_fusion
  422.2 2.2 reshape.339
  424.4 2.1 copy.150
  427.1 5.9 fusion.60
  434.7 4.5 stack.86
  439.2 6.9 fusion.16
  446.2 8.4 %convolution_add_fusion = f32[1280,1088]{0,1:T(8,128)} fusion(f32[1280,1088]{0,1:T(8,128)S(1)} %fusion.16, bf16[1280,1152]{1,0:T(8,128)(2,1)S(1)} %copy-done.13, bf16[3,1152,1088]{2,1,0:T(8,128)(2,1)} %pad.44), kind=kOutput, calls=%fused_computation.12 | convolution fusion | flops 3210035200 | bytes 16744448 | tf_op jit(solution)/shard_map/dot_general | solution.py:510
  454.6 4.1 fusion.61
  463.2 4.2 stack.87
  467.3 4.2 stack.85
  471.5 7.1 maximum_bitcast_fusion.1
  478.6 4.8 copy.117
  483.3 4.1 copy.119
  487.4 7.6 copy.124
  495.0 4.3 fusion.12
  499.3 5.8 multiply_reduce_fusion
  505.9 1.9 subtract_multiply_fusion
  508.0 1.9 convert_element_type.71
  509.9 48.0 %all-reduce.10 = (f32[6,1088]{1,0:T(8,128)S(1)}, f32[1088]{0:T(1024)S(1)}, f32[1088]{0:T(1024)S(1)}, f32[2,8,272]{2,1,0:T(8,128)S(1)}) all-reduce(f32[6,1088]{1,0:T(8,128)S(1)} %stack.97, f32[1088]{0:T(1024)S(1)} %bitcast.211, f32[1088]{0:T(1024)S(1)} %bitcast.212, ...), channel_id=1, replica_groups=mesh['dp'=2,'wide'=8,'narrow'=2] {'dp','wide','narrow'}, use_global_device_ids=true, to_apply=%region_8.9 | all-reduce | flops 13056 | bytes 104448 | tf_op jit(solution)/shard_map/psum | solution.py:999
  561.9 1.9 fusion.53
  566.8 3.7 pad_maximum_fusion.pg
  570.5 2.6 fusion.33
  573.1 2.1 fusion.10
  575.2 1.8 fusion.8
  577.0 1.9 maximum_bitcast_fusion.2
  579.9 3.9 fusion.2
  583.8 3.9 copy.149
  587.7 5.9 reshape.341
  593.6 9.7 %maximum_bitcast_fusion.pa = bf16[2,8,2,304,512]{4,3,2,1,0:T(8,128)(2,1)} fusion(bf16[2,2,8,32,512]{4,3,0,2,1:T(8,128)(2,1)S(1)} %reshape.341, bf16[2,2,8,272,512]{4,3,0,2,1:T(8,128)(2,1)} %fusion.2), kind=kLoop, calls=%fused_computation.11 | loop fusion | flops 19922944 | bytes 19922944 | tf_op jit(solution)/shard_map/transpose | solution.py:974
  603.4 178.9 %shard_map.275 = (f32[2,592,512]{2,1,0:T(8,128)}, f32[2,304,512]{2,1,0:T(8,128)}, bf16[2,272,512]{2,1,0:T(8,128)(2,1)}, bf16[2,272,512]{2,1,0:T(8,128)(2,1)}) custom-call(bf16[8,2,592,512]{3,2,1,0:T(8,128)(2,1)} %get-tuple-element.68.pm, bf16[2,8,2,304,512]{4,3,2,1,0:T(8,128)(2,1)} %maximum_bitcast_fusion.pa, bf16[2,5,272,512]{3,2,1,0:T(8,128)(2,1)} %pad_maximum_fusion.pg, ...), custom_call_target="tpu_custom_call" | custom-call | tf_op jit(solution)/shard_map/pallas_call | solution.py:481
  789.8 3.2 slice.382
  795.8 2.5 reshape.349
  800.8 1.8 pad_maximum_fusion.1
  802.6 2.9 copy.136
  (195 shorter events, 59.9 us)
Async XLA Ops:
  0.6 8.8 %copy-start = (bf16[544,544]{1,0:T(8,128)(2,1)S(1)}, bf16[544,544]{1,0:T(8,128)(2,1)}, u32[]{:S(2)}) copy-start(bf16[544,544]{1,0:T(8,128)(2,1)} %param.33) | copy-start | bytes 1775620
  9.5 2.7 copy-start.19
  12.2 2.4 copy-start.17
  12.5 2.7 copy-start.18
  206.5 4.8 copy-start.12
  249.0 3.2 slice-start.4
  292.8 7.5 slice-start.5
  296.4 4.0 slice-start.6
  300.3 7.7 copy-start.9
  313.8 22.9 %copy-start.4 = (bf16[1152,1088]{1,0:T(8,128)(2,1)S(1)}, bf16[1152,1088]{1,0:T(8,128)(2,1)}, u32[]{:S(2)}) copy-start(bf16[1152,1088]{1,0:T(8,128)(2,1)} %pad.45) | copy-start | bytes 7520260
  339.3 2.6 copy-start.3
  341.9 46.1 %copy-start.5 = (bf16[1152,1088]{1,0:T(8,128)(2,1)S(1)}, bf16[1152,1088]{1,0:T(8,128)(2,1)}, u32[]{:S(2)}) copy-start(bf16[1152,1088]{1,0:T(8,128)(2,1)} %pad.45) | copy-start | bytes 7520260
  417.1 3.6 copy-start.20
  417.1 3.7 copy-start.21
  417.1 3.9 copy-start.7
  417.2 3.9 copy-start.14
  424.4 2.6 copy-start.10
  439.2 6.9 copy-start.13
  446.2 8.4 %copy-start.11 = (bf16[1280,1088]{1,0:T(8,128)(2,1)S(1)}, bf16[1280,1088]{1,0:T(8,128)(2,1)}, u32[]{:S(2)}) copy-start(bf16[1280,1088]{1,0:T(8,128)(2,1)} %copy-done.9) | copy-start | bytes 8355844
  454.6 4.1 copy-start.15
  495.0 10.2 %slice-start = ((s8[5898240]{0:T(1024)(128)(4,1)}), s8[4194304]{0:T(1024)(128)(4,1)S(1)}, s32[]{:S(2)}) async-start(s8[5898240]{0:T(1024)(128)(4,1)} %bitcast.155), calls=%async_computation | async-start | bytes 8388608
  499.3 5.9 slice-start.1
  499.3 6.6 copy-start.2
  505.9 1.9 copy-start.8
  566.8 6.3 slice-start.2
  570.5 2.6 slice-start.3
  784.3 4.4 copy-start.16
  795.8 5.0 copy-start.6
  800.8 4.8 copy-start.1

commit v2 on v1

v2 whole, which is shorter than its diff:
```python
import functools

import jax
import jax.numpy as jnp
from jax import lax
from jax.experimental import pallas as pl
from jax.experimental.pallas import tpu as pltpu
from jax.sharding import PartitionSpec as P

HEAD = 64
REACH = 4
EPS = 1e-05
NEGATIVE = -1e30
LANES = 128
BF = jnp.bfloat16
F32 = jnp.float32
MESH = pl.DeviceIdType.MESH
ANY = pl.BlockSpec(memory_space=pl.ANY)
DMA = pltpu.SemaphoreType.DMA
SCALE = HEAD ** (-0.5)
LIMIT = 60 * 1024 * 1024


def widths(half):
    main = half // LANES * LANES
    return main, half - main


def rem_rows(rows, half):
    main, rem = widths(half)
    return up16(-(-rows // (main // rem)))


def up16(rows):
    return -(-rows // 16) * 16


def pack(block, column=None):
    rows, half = block.shape[-2:]
    main, rem = widths(half)
    count = main // rem
    extra = rem_rows(rows, half)
    lead = block.shape[:-2]
    none = [(0, 0)] * len(lead)
    tail = jnp.pad(block[..., main:], none + [(0, count * extra - rows), (0, 0)])
    tail = jnp.swapaxes(tail.reshape(lead + (count, extra, rem)), -2, -3).reshape(lead + (extra, main))
    if column is not None:
        base, groups = column_base(rows, half), -(-rows // extra)
        column = jnp.pad(column, (0, groups * extra - rows)).reshape(groups, extra).T
        tail = jnp.concatenate([tail[:, :base], column, tail[:, base + groups :]], 1)
    return jnp.concatenate([block[..., :main], tail], -2)


def column_base(rows, half):
    return -(-rows // rem_rows(rows, half)) * widths(half)[1]


def column_of(block, rows, half):
    base, extra = column_base(rows, half), rem_rows(rows, half)
    groups = -(-rows // extra)
    tail = block[..., rows : rows + extra, base : base + groups]
    return jnp.swapaxes(tail, -1, -2).reshape(block.shape[:-2] + (groups * extra,))[..., :rows]


def unpack(block, rows, half):
    main, rem = widths(half)
    count = main // rem
    extra = rem_rows(rows, half)
    lead = block.shape[:-2]
    tail = block[..., rows : rows + extra, :].reshape(lead + (extra, count, rem))
    tail = jnp.swapaxes(tail, -2, -3).reshape(lead + (count * extra, rem))[..., :rows, :]
    return block[..., :rows, :], tail


def unpack_half(block, rows, half):
    return jnp.concatenate(unpack(block, rows, half), -1)


def join(blocks, rows, half):
    body, tail = unpack(blocks, rows, half)
    return jnp.concatenate([body[0], body[1], tail[0], tail[1]], -1)


def halves(full):
    half = full.shape[-1] // 2
    main, rem = widths(half)
    edge = 2 * main
    return jnp.stack(
        [
            jnp.concatenate([full[..., :main], full[..., edge : edge + rem]], -1),
            jnp.concatenate([full[..., main:edge], full[..., edge + rem :]], -1),
        ]
    )


def place():
    c, w, n = lax.axis_index("dp"), lax.axis_index("wide"), lax.axis_index("narrow")
    z, y = lax.div(w, 2), lax.rem(w, 2)
    first = (y + c * (1 - 2 * y), n + (1 - c) * (1 - 2 * n))
    second = (y + (1 - c) * (1 - 2 * y), n + c * (1 - 2 * n))
    return c, z, y, n, first, second


def wide_of(z, y):
    return z * 2 + y


def remote(src, dst, send, recv, device):
    return pltpu.make_async_remote_copy(
        src_ref=src, dst_ref=dst, send_sem=send, recv_sem=recv, device_id=device, device_id_type=MESH
    )


def greet(devices):
    barrier = pltpu.get_barrier_semaphore()
    for device in devices:
        pl.semaphore_signal(barrier, inc=1, device_id=device, device_id_type=MESH)
    pl.semaphore_wait(barrier, len(devices))


def partners(outer):
    c, z, y, n, _, _ = place()
    out = [(c, wide_of(lax.rem(z + d, outer), y), n) for d in range(1, outer)]
    out.append((c, wide_of(z, 1 - y), n))
    out.append((c, wide_of(z, y), 1 - n))
    out.append((1 - c, wide_of(z, y), n))
    return out


class Gather:
    def __init__(self, outer, src, out, both, first, second, sems):
        self.outer, self.src, self.out, self.both = outer, src, out, both
        self.first, self.second = first, second
        self.zs, self.zr, self.fs, self.fr, self.ss, self.sr, self.cs, self.cr, self.local = sems
        self.sent = []

    def block(self, z, y, n):
        c = lax.axis_index("dp")
        return self.out.at[c, wide_of(z, y), n] if self.both else self.out.at[wide_of(z, y), n]

    def go(self, copy):
        copy.start()
        self.sent.append(copy)

    def z_at(self, d):
        return lax.rem(place()[1] + self.outer - d, self.outer)

    def to_first(self, d, src):
        c, z, y, n, _, _ = place()
        first, second = self.first, self.second
        device = (c, wide_of(z, first[0]), first[1])
        self.go(remote(src, self.block(self.z_at(d), y, n), self.fs.at[d], self.fr.at[d], device))

    def to_second(self, d, src, k):
        c, z, y, n, _, _ = place()
        first, second = self.first, self.second
        device = (c, wide_of(z, second[0]), second[1])
        dst = self.block(self.z_at(d), y, n) if k == 0 else self.block(self.z_at(d), *first)
        i = k * self.outer + d
        self.go(remote(src, dst, self.ss.at[i], self.sr.at[i], device))

    def to_core(self, i, src, dst):
        if self.both:
            c, z, y, n, _, _ = place()
            self.go(remote(src, dst, self.cs.at[i], self.cr.at[i], (1 - c, wide_of(z, y), n)))

    def start(self):
        c, z, y, n, _, _ = place()
        first, second = self.first, self.second
        own = self.block(z, y, n)
        self.keep = pltpu.make_async_copy(self.src, own, self.local)
        self.keep.start()
        for d in range(1, self.outer):
            device = (c, wide_of(lax.rem(z + d, self.outer), y), n)
            self.go(remote(self.src, own, self.zs.at[d - 1], self.zr.at[d - 1], device))

    def start_rest(self):
        c, z, y, n, _, _ = place()
        own = self.block(z, y, n)
        self.to_first(0, self.src)
        self.to_second(0, self.src, 0)
        self.to_core(0, self.src, own)

    def arrived(self, dst, recv):
        c, z, y, n, _, _ = place()
        remote(dst, dst, recv, recv, (1 - c, wide_of(z, y), n)).wait_recv()

    def along_z(self, d):
        c, z, y, n, _, _ = place()
        first, second = self.first, self.second
        got = self.block(self.z_at(d), y, n)
        self.arrived(got, self.zr.at[d - 1])
        self.to_first(d, got)
        self.to_second(d, got, 0)
        self.to_core(d, got, got)

    def along_first(self, d):
        c, z, y, n, _, _ = place()
        first, second = self.first, self.second
        got = self.block(self.z_at(d), *first)
        self.arrived(got, self.fr.at[d])
        self.to_second(d, got, 1)
        self.to_core(self.outer + d, got, got)

    def along_second(self, d, k):
        c, z, y, n, _, _ = place()
        first, second = self.first, self.second
        got = self.block(self.z_at(d), *second) if k == 0 else self.block(self.z_at(d), 1 - y, 1 - n)
        i = k * self.outer + d
        self.arrived(got, self.sr.at[i])
        self.to_core(2 * self.outer + i, got, got)

    def finish(self):
        c, z, y, n, _, _ = place()
        first, second = self.first, self.second
        if self.both:
            spots = [(y, n), first, second, (1 - y, 1 - n)]
            for k, spot in enumerate(spots):
                for d in range(self.outer):
                    got = self.out.at[1 - c, wide_of(self.z_at(d), spot[0]), spot[1]]
                    self.arrived(got, self.cr.at[k * self.outer + d])
        self.keep.wait()
        for copy in self.sent:
            copy.wait_send()


def gather_sems(outer):
    return [
        DMA((outer,)),
        DMA((outer,)),
        DMA((outer,)),
        DMA((outer,)),
        DMA((2 * outer,)),
        DMA((2 * outer,)),
        DMA((4 * outer,)),
        DMA((4 * outer,)),
        DMA,
    ]


class Scatter:
    def __init__(self, outer, part, value, one, two, three, fin, sems):
        self.outer, self.part, self.value = outer, part, value
        self.one, self.two, self.three, self.fin = one, two, three, fin
        self.ss, self.sr, self.fs, self.fr, self.zs, self.zr, self.cs, self.cr = sems
        self.sent = []

    def go(self, copy):
        copy.start()
        self.sent.append(copy)

    def arrived(self, dst, recv):
        c, z, y, n, _, _ = place()
        remote(dst, dst, recv, recv, (1 - c, wide_of(z, y), n)).wait_recv()

    def z_at(self, d):
        return lax.rem(place()[1] + d, self.outer)

    def order(self):
        return [d for d in range(1, self.outer)] + [0]

    def start(self):
        c, z, y, n, first, second = place()
        device = (c, wide_of(z, second[0]), second[1])
        for k, spot in ((1, (1 - y, 1 - n)), (0, second)):
            for d in self.order():
                i = k * self.outer + d
                self.go(
                    remote(self.part(self.z_at(d), *spot), self.one.at[i], self.ss.at[i], self.sr.at[i], device)
                )

    def to_first(self, d):
        c, z, y, n, first, second = place()
        device = (c, wide_of(z, first[0]), first[1])
        i = self.outer + d
        own = self.value(self.z_at(d), *first)
        self.arrived(self.one.at[i], self.sr.at[i])
        self.one[i] = (self.one[i].astype(F32) + own.astype(F32)).astype(BF)
        self.go(remote(self.one.at[i], self.two.at[d], self.fs.at[d], self.fr.at[d], device))

    def to_z(self, d):
        c, z, y, n, first, second = place()
        own = self.value(self.z_at(d), y, n)
        self.arrived(self.one.at[d], self.sr.at[d])
        self.arrived(self.two.at[d], self.fr.at[d])
        half = (self.one[d].astype(F32) + own.astype(F32)).astype(BF).astype(F32)
        value = half + self.two[d].astype(F32)
        if d == 0:
            self.fin[c] = value
        else:
            self.one[d] = value.astype(BF)
            device = (c, wide_of(self.z_at(d), y), n)
            self.go(
                remote(self.one.at[d], self.three.at[d - 1], self.zs.at[d - 1], self.zr.at[d - 1], device)
            )

    def close(self):
        c, z, y, n, first, second = place()
        for d in range(1, self.outer):
            self.arrived(self.three.at[d - 1], self.zr.at[d - 1])
        value = self.fin[c]
        for d in range(1, self.outer):
            value = value + self.three[d - 1].astype(F32)
        self.fin[c] = value
        self.go(remote(self.fin.at[c], self.fin.at[c], self.cs, self.cr, (1 - c, wide_of(z, y), n)))

    def finish(self):
        c = lax.axis_index("dp")
        self.arrived(self.fin.at[1 - c], self.cr)
        for copy in self.sent:
            copy.wait_send()


def scatter_scratch(outer, block):
    return [
        pltpu.VMEM((2 * outer,) + block, BF),
        pltpu.VMEM((outer,) + block, BF),
        pltpu.VMEM((max(outer - 1, 1),) + block, BF),
    ]


def scatter_sems(outer):
    return [
        DMA((2 * outer,)),
        DMA((2 * outer,)),
        DMA((outer,)),
        DMA((outer,)),
        DMA((outer,)),
        DMA((outer,)),
        DMA,
        DMA,
    ]


def leave_kernel(
    outer, hc, rem, dq, dk, dv, low1, mixed, branch, sums, pg, lo,
    ao, xg, lo_out, vec_out,
    pa, pcore, full, edge, acc, got_x, got_z, got_y, a1, a2, a3, vx, vz, xs, xr, ccs, ccr, vs, vr, *sems
):
    c, z, y, n, first, second = place()
    me = wide_of(z, y)
    wide = 2 * outer
    greet(partners(outer))
    other_n = (c, me, 1 - n)
    other_y = (c, wide_of(z, 1 - y), n)
    other_c = (1 - c, me, n)
    earlier = (c, wide_of(lax.rem(z + outer - 1, outer), y), n)
    sent = []
    main = pa.shape[4]
    rows = dq.shape[0]
    span = dk.shape[0]
    cols = 2 * hc
    padded = dq.shape[1]
    block_rows = edge.shape[2]
    extra = pa.shape[3] - block_rows

    def go(copy):
        copy.start()
        sent.append(copy)

    def arrived(dst, recv):
        remote(dst, dst, recv, recv, other_c).wait_recv()

    def products(s, left, right):
        size = 256
        for begin in range(0, padded, size):
            stop = min(begin + size, padded)
            full[s, begin:stop, :] = dot(left[:, begin:stop], right, TN).astype(BF)

    go(remote(pg.at[1 - n], got_x, xs.at[0], xr.at[0], other_n))
    vx[0] = sums[...]
    go(remote(vx.at[0], vx.at[1], vs.at[0], vr.at[0], other_n))
    acc[...] = jnp.zeros_like(acc)
    for j in range(5):
        acc[n + j] = pg[n, j].astype(F32)
    products(3, mixed, branch[...])
    products(0, dq, low1[span - rows :, :])
    vx_sum = sums[...]
    arrived(vx.at[1], vr.at[0])
    vx_sum = vx_sum + vx[1]
    vx[2] = vx_sum
    go(remote(vx.at[2], vx.at[3], vs.at[1], vr.at[1], other_y))
    products(1, dk, low1[...])
    arrived(vx.at[3], vr.at[1])
    vx_sum = vx[2] + vx[3]
    vx[4] = vx_sum
    go(remote(vx.at[4], vx.at[5], vs.at[2], vr.at[2], other_c))
    arrived(got_x, xr.at[0])
    for j in range(5):
        acc[1 - n + j] = acc[1 - n + j] + got_x[j].astype(F32)
    got_x[pl.ds(0, 2)] = acc[pl.ds(2, 2)].astype(BF)
    go(remote(got_x.at[pl.ds(0, 2)], got_y, xs.at[1], xr.at[1], other_y))
    products(2, dv, low1[...])
    arrived(vx.at[5], vr.at[2])
    vz[z] = vx[4] + vx[5]
    for d in range(1, outer):
        device = (c, wide_of(lax.rem(z + d, outer), y), n)
        go(remote(vz.at[z], vz.at[z], vs.at[2 + d], vr.at[2 + d], device))

    def place_rows(half):
        for i in range(wide):
            for s in range(4):
                to = slice(s * hc, (s + 1) * hc)
                src = slice(i * cols, i * cols + hc)
                src = pl.ds(i * cols + half * hc, hc)
                for h in range(2):
                    pa[half, i, h, to, :] = full[s, src, h * main : (h + 1) * main]
                edge[half, i, to, :] = full[s, src, 2 * main :]
            if block_rows > 4 * hc:
                gap = slice(4 * hc, block_rows)
                for h in range(2):
                    pa[half, i, h, gap, :] = jnp.zeros((block_rows - 4 * hc, main), BF)
                edge[half, i, gap, :] = jnp.zeros((block_rows - 4 * hc, LANES), BF)
            low = edge[half, i].astype(F32)
            for h in range(2):
                pa[half, i, h, block_rows:, :] = squeezed(
                    low[:, h * rem : (h + 1) * rem], extra, main, low[:, 2 * rem : 2 * rem + 1]
                ).astype(BF)

    core_copies = [remote(pa.at[1 - c], pcore, ccs, ccr, other_c)]
    place_rows(0)
    place_rows(1)
    core_copies[0].start()
    arrived(got_y, xr.at[1])
    spot = pl.ds(4 * (1 - y), 2)
    acc[spot] = acc[spot] + got_y[...].astype(F32)
    got_x[pl.ds(2, 2)] = acc[pl.ds(0, 2)].astype(BF)
    go(remote(got_x.at[pl.ds(2, 2)], got_z, xs.at[2], xr.at[2], earlier))
    core_copies[0].wait_recv()

    @pl.loop(0, wide)
    def _(i):
        for h in range(2):
            pcore[i, h] = (pcore[i, h].astype(F32) + pa[c, i, h].astype(F32)).astype(BF)

    ref = lambda z, y, n: pcore.at[wide_of(z, y), n]
    heads = Scatter(outer, ref, lambda z, y, n: pcore[wide_of(z, y), n], a1, a2, a3, ao, sems)
    heads.start()
    go(remote(lo.at[1 - n], lo_out.at[n], xs.at[3], xr.at[3], other_n))
    lo_out[n] = lo[n]
    for d in heads.order():
        heads.to_first(d)
    for d in heads.order():
        heads.to_z(d)
    arrived(got_z, xr.at[2])
    xg[...] = (acc[pl.ds(4, 2)] + got_z[...].astype(F32)).astype(BF)
    for d in range(1, outer):
        arrived(vz.at[lax.rem(z + outer - d, outer)], vr.at[2 + d])
    total = vz[0]
    for i in range(1, outer):
        total = total + vz[i]
    vec_out[...] = total
    heads.close()
    arrived(lo_out.at[1 - n], xr.at[3])
    core_copies[0].wait_send()
    for copy in sent:
        copy.wait_send()
    heads.finish()


def leave(dq, dk, dv, low1, mixed, branch, sums, pg, lo, hc, rem):
    wide = lax.axis_size("wide")
    outer = wide // 2
    main = lo.shape[2]
    bx = lo.shape[1:]
    block_rows = up16(4 * hc)
    ba = (block_rows + rem_rows(block_rows, main + rem), main)
    padded = dq.shape[1]
    vmem = pl.BlockSpec(memory_space=pltpu.VMEM)
    return pl.pallas_call(
        functools.partial(leave_kernel, outer, hc, rem),
        out_shape=(
            jax.ShapeDtypeStruct((2,) + ba, F32),
            jax.ShapeDtypeStruct((2,) + bx, BF),
            jax.ShapeDtypeStruct((2,) + bx, BF),
            jax.ShapeDtypeStruct(sums.shape, F32),
        ),
        in_specs=[vmem] * 9,
        out_specs=(vmem,) * 4,
        scratch_shapes=[
            pltpu.VMEM((2, wide, 2) + ba, BF),
            pltpu.VMEM((wide, 2) + ba, BF),
            pltpu.VMEM((4, padded, padded), BF),
            pltpu.VMEM((2, wide, block_rows, LANES), BF),
            pltpu.VMEM((6,) + bx, F32),
            pltpu.VMEM((5,) + bx, BF),
            pltpu.VMEM((2,) + bx, BF),
            pltpu.VMEM((2,) + bx, BF),
        ]
        + scatter_scratch(outer, ba)
        + [pltpu.VMEM((6,) + sums.shape, F32), pltpu.VMEM((outer,) + sums.shape, F32)]
        + [DMA((4,)), DMA((4,)), DMA, DMA, DMA((2 + outer,)), DMA((2 + outer,))]
        + scatter_sems(outer),
        compiler_params=pltpu.CompilerParams(
            collective_id=1, has_side_effects=True, vmem_limit_bytes=LIMIT
        ),
    )(dq, dk, dv, low1, mixed, branch, sums, pg, lo)


def dot(left, right, dims):
    return lax.dot_general(left, right, ((dims[0], dims[1]), ((), ())), preferred_element_type=F32)


NN = ((1,), (0,))
NT = ((1,), (1,))
TN = ((0,), (0,))


def spread(tail, rows, rem):
    extra = tail.shape[0]
    count = -(-rows // extra)
    return jnp.concatenate([tail[:, k * rem : (k + 1) * rem] for k in range(count)], 0)[:rows]


def squeezed(block, extra, main, column=None):
    parts = []
    for piece in (block,) if column is None else (block, column):
        rows, each = piece.shape
        count = -(-rows // extra)
        short = count * extra - rows
        if short:
            piece = jnp.concatenate([piece, jnp.zeros((short, each), piece.dtype)], 0)
        parts += [piece[k * extra : (k + 1) * extra] for k in range(count)]
    used = sum(p.shape[1] for p in parts)
    if used < main:
        parts.append(jnp.zeros((extra, main - used), block.dtype))
    return jnp.concatenate(parts, 1)


def store_packed(ref, index, value, main, rem):
    rows = value.shape[0]
    for h in range(2):
        at = ref.at[(h,) + index]
        at[0:rows, :] = value[:, h * main : (h + 1) * main].astype(ref.dtype)
        low = value[:, 2 * main + h * rem : 2 * main + (h + 1) * rem]
        at[rows:, :] = squeezed(low, at.shape[0] - rows, main).astype(ref.dtype)


def gelu_and_slope(u):
    share = 0.5 * (1.0 + lax.erf(u * 0.7071067811865476))
    return u * share, share + u * (jnp.exp(-0.5 * u * u) * 0.3989422804014327)


def mlp_kernel(
    wide, fc, rem, low2, cot_in, gm, residual, vec,
    pm, lo, grad_res, sums,
    weights, grads, tails, cot, low2_all, acc, got, wsem, tsem, psem, qsem, xs, xr
):
    c, w, n = lax.axis_index("dp"), lax.axis_index("wide"), lax.axis_index("narrow")
    other = (1 - c, w, n)
    rows, padded = low2.shape
    main = gm.shape[3]
    width = 2 * (main + rem)
    extra = gm.shape[2] - 2 * fc
    nf = wide * fc
    base = -(-2 * fc // extra) * rem
    greet([other])
    mine, theirs = pl.ds(c * rows, rows), pl.ds((1 - c) * rows, rows)
    swap_low = remote(low2, low2_all.at[mine], xs.at[0], xr.at[0], other)
    swap_low.start()

    def weight_copies(i):
        out = []
        for h in range(2):
            for k in range(2):
                out.append(
                    pltpu.make_async_copy(
                        gm.at[i, h, pl.ds(k * fc, fc)],
                        weights.at[k, pl.ds(i * fc, fc), pl.ds(h * main, main)],
                        wsem.at[i, h, k],
                    )
                )
            out.append(pltpu.make_async_copy(gm.at[i, h, pl.ds(2 * fc, extra)], tails.at[i, h], tsem.at[i, h]))
        return out

    @pl.loop(0, wide)
    def _(i):
        for copy in weight_copies(i):
            copy.start()

    low2_all[mine] = low2[...]
    for k in range(2):
        span = slice(k * rows, (k + 1) * rows)
        for h in range(2):
            cot[span, h * main : (h + 1) * main] = cot_in[k, h, 0:rows, :]
        cot[span, 2 * main :] = edge_tile([cot_in[k, h, rows:, :] for h in range(2)], rows, rem)

    @pl.loop(0, wide)
    def _(i):
        for copy in weight_copies(i):
            copy.wait()
        both = edge_tile([tails[i, h] for h in range(2)], 2 * fc, rem, base)
        for k in range(2):
            weights[k, pl.ds(i * fc, fc), 2 * main :] = both[k * fc : (k + 1) * fc]

    acc[...] = jnp.zeros_like(acc)
    swap_low.wait_recv()

    def step(start, size):
        at = pl.ds(start, size)
        before = dot(low2_all[...], weights[0, at, :], NT)
        hidden, slope = gelu_and_slope(before)
        hidden = hidden.astype(BF)
        acc[0] += dot(hidden, weights[1, at, :], NN)
        grads[1, at, :] = dot(hidden, cot[...], TN).astype(BF)
        grad = dot(cot[...], weights[1, at, :], NT) * slope
        grad = grad.astype(BF)
        acc[1] += dot(grad, weights[0, at, :], NN)
        grads[0, at, :] = dot(grad, low2_all[...], TN).astype(BF)

    size = 256
    full = nf // size

    @pl.loop(0, full)
    def _(j):
        step(pl.multiple_of(j * size, size), size)

    if nf % size:
        step(full * size, nf % size)

    swap_acc = remote(acc.at[:, theirs], got, xs.at[1], xr.at[1], other)
    swap_acc.start()

    def grad_copies(i):
        out = []
        for h in range(2):
            for k in range(2):
                out.append(
                    pltpu.make_async_copy(
                        grads.at[k, pl.ds(i * fc, fc), pl.ds(h * main, main)],
                        pm.at[i, h, pl.ds(k * fc, fc)],
                        psem.at[i, h, k],
                    )
                )
        return out

    def tail_copies(i):
        return [
            pltpu.make_async_copy(tails.at[i, h], pm.at[i, h, pl.ds(2 * fc, extra)], qsem.at[i, h])
            for h in range(2)
        ]

    @pl.loop(0, wide)
    def _(i):
        for copy in grad_copies(i):
            copy.start()
        low = jnp.concatenate([grads[k, pl.ds(i * fc, fc), 2 * main :] for k in range(2)], 0).astype(F32)
        for h in range(2):
            tails[i, h] = squeezed(low[:, h * rem : (h + 1) * rem], extra, main, low[:, 2 * rem : 2 * rem + 1]).astype(BF)
        for copy in tail_copies(i):
            copy.start()

    swap_acc.wait_recv()
    result = residual[...] + (acc[0, mine] + got[0]) + vec[5:6]
    store_packed(lo, (), result, main, rem)
    normed2, scale2 = normed_rows(residual[...], width)
    grad_low2 = acc[1, mine] + got[1]
    grad_out = cot[mine].astype(F32)
    lane = lax.broadcasted_iota(jnp.int32, grad_out.shape, 1)
    total = jnp.where(lane < width, grad_out + norm_back(grad_low2, normed2, scale2, vec[3:4], width), 0.0)
    grad_res[...] = total
    sums[...] = jnp.zeros_like(sums)
    sums[2:3] = jnp.sum(total.astype(BF).astype(F32), 0, keepdims=True)
    sums[3:4] = jnp.sum(grad_low2 * normed2, 0, keepdims=True)
    sums[4:5] = jnp.sum(grad_low2, 0, keepdims=True)
    sums[5:6] = jnp.sum(grad_out, 0, keepdims=True)

    @pl.loop(0, wide)
    def _(i):
        for copy in grad_copies(i) + tail_copies(i):
            copy.wait()

    swap_low.wait_send()
    swap_acc.wait_send()


def mlp(low2, cot_in, gm, residual, vec, fc, rem):
    wide = gm.shape[0]
    rows, padded = low2.shape
    nf = wide * fc
    main = gm.shape[3]
    extra = gm.shape[2] - 2 * fc
    vmem = pl.BlockSpec(memory_space=pltpu.VMEM)
    return pl.pallas_call(
        functools.partial(mlp_kernel, wide, fc, rem),
        out_shape=(
            jax.ShapeDtypeStruct(gm.shape, BF),
            jax.ShapeDtypeStruct((2,) + cot_in.shape[2:], BF),
            jax.ShapeDtypeStruct((rows, padded), F32),
            jax.ShapeDtypeStruct((16, padded), F32),
        ),
        in_specs=[vmem, vmem, ANY, vmem, vmem],
        out_specs=(ANY, vmem, vmem, vmem),
        scratch_shapes=[
            pltpu.VMEM((2, nf, padded), BF),
            pltpu.VMEM((2, nf, padded), BF),
            pltpu.VMEM((wide, 2, extra, main), BF),
            pltpu.VMEM((2 * rows, padded), BF),
            pltpu.VMEM((2 * rows, padded), BF),
            pltpu.VMEM((2, 2 * rows, padded), F32),
            pltpu.VMEM((2, rows, padded), F32),
            DMA((wide, 2, 2)),
            DMA((wide, 2)),
            DMA((wide, 2, 2)),
            DMA((wide, 2)),
            DMA((2,)),
            DMA((2,)),
        ],
        compiler_params=pltpu.CompilerParams(
            collective_id=2, has_side_effects=True, vmem_limit_bytes=LIMIT
        ),
    )(low2, cot_in, gm, residual, vec)


def fill_mask(q_seg, k_seg, mask):
    keys, queries = mask.shape
    key = lax.broadcasted_iota(jnp.int32, (keys, queries), 0)
    query = lax.broadcasted_iota(jnp.int32, (keys, queries), 1) + (keys - queries)
    allowed = (k_seg[...] == q_seg[...]) & (key <= query)
    mask[...] = jnp.where(allowed, 0.0, NEGATIVE)


def turned(block):
    return block.astype(F32).T


def attend_pair(q, k, v, mask):
    q_t = turned(q) * SCALE
    row = lax.broadcasted_iota(jnp.int32, q_t.shape, 0)
    parts, logs = [], []
    for h in range(2):
        mine = (row >= h * HEAD) & (row < (h + 1) * HEAD)
        s = dot(k, jnp.where(mine, q_t, 0.0).astype(BF), NN) + mask[...]
        top = jnp.max(s, 0, keepdims=True)
        p = jnp.exp(s - top)
        total = jnp.sum(p, 0, keepdims=True)
        p = (p * (1.0 / total)).astype(BF)
        parts.append(dot(v, p, TN)[h * HEAD : (h + 1) * HEAD])
        logs.append(top + jnp.log(total))
    return jnp.concatenate(parts, 0).T.astype(BF), logs


def normed_rows(values, width):
    lane = lax.broadcasted_iota(jnp.int32, values.shape, 1)
    mean = jnp.sum(values, 1, keepdims=True) * (1.0 / width)
    centred = jnp.where(lane < width, values - mean, 0.0)
    scale = lax.rsqrt(jnp.sum(centred * centred, 1, keepdims=True) * (1.0 / width) + EPS)
    return centred * scale, scale


def norm_back(grad, normed, scale, gain, width):
    lane = lax.broadcasted_iota(jnp.int32, grad.shape, 1)
    scaled = jnp.where(lane < width, grad * gain, 0.0)
    first = jnp.sum(scaled, 1, keepdims=True) * (1.0 / width)
    second = jnp.sum(scaled * normed, 1, keepdims=True) * (1.0 / width)
    return scale * (scaled - first - normed * second)


def edge_tile(tails, rows, rem, base=None):
    tails = [t.astype(F32) for t in tails]
    parts = [spread(t, rows, rem) for t in tails]
    used = 2 * rem
    if base is not None:
        parts.append(spread(tails[0][:, base:], rows, 1))
        used += 1
    parts.append(jnp.zeros((rows, LANES - used), F32))
    return jnp.concatenate(parts, 1).astype(BF)


def forward_kernel(
    outer, hc, rem, xin, cot, sa, sm, q_seg, k_seg,
    cot_out, gm, wa_out, x_out, low1_out, k_out, v_out, q, mixed, lse, residual, low2, vec,
    ga, xs6, wa, x5, low1, k, v, mask, xs, xr, hs, hr, ks, kr, ls, os, *sems
):
    c, z, y, n, first, second = place()
    me = wide_of(z, y)
    wide = 2 * outer
    greet(partners(outer))
    other_n = (c, me, 1 - n)
    other_y = (c, wide_of(z, 1 - y), n)
    other_c = (1 - c, me, n)
    later = (c, wide_of(lax.rem(z + 1, outer), y), n)
    main = sa.shape[1]
    width = 2 * (main + rem)
    rows = q.shape[0]
    span = x5.shape[0]
    cols = 2 * hc
    sent = []

    def go(copy):
        copy.start()
        sent.append(copy)

    def arrived(dst, recv):
        remote(dst, dst, recv, recv, other_c).wait_recv()

    def x_send(j):
        src = xs6.at[n, j + 1 - n] if j < 4 else xin.at[1 - n]
        go(remote(src, xs6.at[n, j + 1 - n], hs.at[j], hr.at[j], other_n))

    own = xs6.at[n, pl.ds(4, 2)]
    keep = pltpu.make_async_copy(xin, own, ls.at[0])
    keep.start()
    keep_cot = pltpu.make_async_copy(cot.at[n], cot_out.at[c, n], ls.at[1])
    keep_cot.start()
    go(remote(xin, xs6.at[n, pl.ds(0, 2)], xs.at[0], xr.at[0], later))
    x_send(4)
    heads = Gather(outer, sa, ga, True, (y, 1 - n), (1 - y, n), sems[:9])
    heads.start()
    heads.start_rest()
    fill_mask(q_seg, k_seg, mask)
    wa[:, width:, :] = jnp.zeros((4, wa.shape[1] - width, wa.shape[2]), BF)
    arrived(xs6.at[n, pl.ds(0, 2)], xr.at[0])
    keep.wait()
    x_send(0)
    go(remote(xs6.at[n, pl.ds(4 * (1 - y), 2)], xs6.at[n, pl.ds(2, 2)], xs.at[1], xr.at[1], other_y))
    for d in range(1, outer):
        heads.along_z(d)
    feed = Gather(outer, sm, gm, False, first, second, sems[9:])
    feed.start()
    arrived(xs6.at[n, pl.ds(2, 2)], xr.at[1])
    for j in (1, 2, 3):
        x_send(j)
    for d in range(outer):
        heads.along_first(d)
    go(remote(cot.at[1 - n], cot_out.at[c, n], ks.at[0], kr.at[0], other_n))
    go(remote(cot.at[n], cot_out.at[c, n], ks.at[1], kr.at[1], other_c))
    feed.start_rest()

    for j in range(5):
        arrived(xs6.at[1 - n, j + n], hr.at[j])
    for j in range(5):
        at = slice(j * rows, (j + 1) * rows)
        for h in range(2):
            x5[at, h * main : (h + 1) * main] = xs6[h, n + j, 0:rows, :]
        x5[at, 2 * main :] = edge_tile([xs6[h, n + j, rows:, :] for h in range(2)], rows, rem)
    outs = [pltpu.make_async_copy(x5, x_out, os.at[0])]
    outs[0].start()
    for kk in range(2):
        for d in range(outer):
            heads.along_second(d, kk)
    heads.finish()
    for d in range(1, outer):
        feed.along_z(d)

    block_rows = 16 + up16(4 * hc)
    extra = ga.shape[3] - block_rows
    base = -(-block_rows // extra) * rem
    for i in range(wide):
        for half in range(2):
            edge = edge_tile([ga[half, i, h, block_rows:, :] for h in range(2)], block_rows, rem, base)
            for s in range(4):
                src = slice(s * hc, (s + 1) * hc)
                to = slice(i * cols + half * hc, i * cols + (half + 1) * hc)
                for h in range(2):
                    wa[s, to, h * main : (h + 1) * main] = ga[half, i, h, src, :]
                wa[s, to, 2 * main :] = edge[src]
            if i == 0 and half == 0:
                at = slice(block_rows - 16, block_rows)
                for h in range(2):
                    vec[:, h * main : (h + 1) * main] = ga[0, 0, h, at, :].astype(F32)
                vec[:, 2 * main :] = edge[at].astype(F32)
    outs.append(pltpu.make_async_copy(wa, wa_out, os.at[1]))
    outs[1].start()

    @pl.loop(0, span // rows)
    def _(j):
        at = pl.ds(pl.multiple_of(j * rows, rows), rows)
        normed, _ = normed_rows(x5[at, :].astype(F32), width)
        low1[at, :] = (normed * vec[0:1] + vec[1:2]).astype(BF)
        k[at, :] = dot(low1[at, :], wa[1], NT).astype(BF)
        v[at, :] = dot(low1[at, :], wa[2], NT).astype(BF)

    q[...] = dot(low1[span - rows :, :], wa[0], NT).astype(BF)
    for src, dst in ((low1, low1_out), (k, k_out), (v, v_out)):
        outs.append(pltpu.make_async_copy(src, dst, os.at[len(outs)]))
        outs[-1].start()

    pairs = q.shape[1] // LANES
    lse[...] = jnp.zeros_like(lse)

    def some(begin, end):
        @pl.loop(begin, end)
        def _(i):
            at = pl.ds(pl.multiple_of(i * LANES, LANES), LANES)
            out, logs = attend_pair(q[:, at], k[:, at], v[:, at], mask)
            mixed[:, at] = out
            for h in range(2):
                lse[i, pl.ds(h, 1), :] = logs[h]

    cut = pairs // 2
    some(0, cut)
    for d in range(outer):
        feed.along_first(d)
    arrived(cot_out.at[c, 1 - n], kr.at[0])
    go(remote(cot_out.at[c, 1 - n], cot_out.at[c, 1 - n], ks.at[2], kr.at[2], other_c))
    some(cut, pairs)
    value = x5[span - rows :, :].astype(F32) + dot(mixed[...], wa[3], NN) + vec[2:3]
    residual[...] = value
    normed, _ = normed_rows(value, width)
    low2[...] = (normed * vec[3:4] + vec[4:5]).astype(BF)

    for kk in range(2):
        for d in range(outer):
            feed.along_second(d, kk)
    arrived(cot_out.at[1 - c, n], kr.at[1])
    arrived(cot_out.at[1 - c, 1 - n], kr.at[2])
    keep_cot.wait()
    for copy in outs:
        copy.wait()
    for copy in sent:
        copy.wait_send()
    feed.finish()


def forward(xin, cot, sa, sm, q_seg, k_seg, hc, rem):
    wide = lax.axis_size("wide")
    outer = wide // 2
    main = sa.shape[1]
    width = 2 * (main + rem)
    padded = -(-(width + 1) // LANES) * LANES
    rows = q_seg.shape[1]
    span = k_seg.shape[0]
    pairs = padded // LANES
    vmem = pl.BlockSpec(memory_space=pltpu.VMEM)
    shape = jax.ShapeDtypeStruct
    return pl.pallas_call(
        functools.partial(forward_kernel, outer, hc, rem),
        out_shape=(
            shape((2,) + cot.shape, BF),
            shape((wide, 2) + sm.shape, BF),
            shape((4, padded, padded), BF),
            shape((span, padded), BF),
            shape((span, padded), BF),
            shape((span, padded), BF),
            shape((span, padded), BF),
            shape((rows, padded), BF),
            shape((rows, padded), BF),
            shape((pairs, 8, rows), F32),
            shape((rows, padded), F32),
            shape((rows, padded), BF),
            shape((16, padded), F32),
        ),
        in_specs=[ANY] * 4 + [vmem] * 2,
        out_specs=(ANY,) * 7 + (vmem,) * 6,
        scratch_shapes=[
            pltpu.VMEM((2, wide, 2) + sa.shape, BF),
            pltpu.VMEM((2, 6) + xin.shape[1:], BF),
            pltpu.VMEM((4, padded, padded), BF),
            pltpu.VMEM((span, padded), BF),
            pltpu.VMEM((span, padded), BF),
            pltpu.VMEM((span, padded), BF),
            pltpu.VMEM((span, padded), BF),
            pltpu.VMEM((span, rows), F32),
        ]
        + [DMA((2,)), DMA((2,)), DMA((5,)), DMA((5,)), DMA((3,)), DMA((3,)), DMA((2,)), DMA((5,))]
        + gather_sems(outer)
        + gather_sems(outer),
        compiler_params=pltpu.CompilerParams(
            collective_id=0, has_side_effects=True, vmem_limit_bytes=LIMIT
        ),
    )(xin, cot, sa, sm, q_seg, k_seg)


def attend_back_pair(q, k, v, g, lse, mask):
    q_n = q.astype(F32) * SCALE
    g_n = g.astype(F32)
    q_t, g_t = q_n.T, g_n.T
    row = lax.broadcasted_iota(jnp.int32, q_t.shape, 0)
    lane = lax.broadcasted_iota(jnp.int32, q_n.shape, 1)
    parts = []
    dk_sum = dv_sum = None
    for h in range(2):
        in_row = (row >= h * HEAD) & (row < (h + 1) * HEAD)
        in_lane = (lane >= h * HEAD) & (lane < (h + 1) * HEAD)
        s = dot(k, jnp.where(in_row, q_t, 0.0).astype(BF), NN) + mask[...]
        p = jnp.exp(s - lse[h : h + 1])
        dp = dot(v, jnp.where(in_row, g_t, 0.0).astype(BF), NN)
        delta = jnp.sum(p * dp, 0, keepdims=True)
        ds = (p * (dp - delta)).astype(BF)
        one = dot(ds, jnp.where(in_lane, q_n, 0.0).astype(BF), NN)
        two = dot(p.astype(BF), jnp.where(in_lane, g_n, 0.0).astype(BF), NN)
        dk_sum = one if dk_sum is None else dk_sum + one
        dv_sum = two if dv_sum is None else dv_sum + two
        parts.append(dot(k, ds, TN)[h * HEAD : (h + 1) * HEAD] * SCALE)
    return jnp.concatenate(parts, 0).T.astype(BF), dk_sum.astype(BF), dv_sum.astype(BF)


def backward_kernel(
    outer, rem, grad_res, q, lse, q_seg, k_seg, vec, sums_in, k_in, v_in, wa_in, x_in, pm,
    mo, dq, dk, dv, pg, branch, sums,
    w, k, v, x5, g, mask, stage, m1, m2, m3, ls, st, *sems
):
    greet(partners(outer))
    main = pm.shape[3]
    width = 2 * (main + rem)
    rows, padded = q.shape
    span = k.shape[0]

    def value(z, y, n):
        copy = pltpu.make_async_copy(pm.at[wide_of(z, y), n], stage, st)
        copy.start()
        copy.wait()
        return stage[...]

    feed = Scatter(outer, lambda z, y, n: pm.at[wide_of(z, y), n], value, m1, m2, m3, mo, sems)
    loads = [
        pltpu.make_async_copy(src, dst, ls.at[i])
        for i, (src, dst) in enumerate(
            (
                (wa_in.at[3], w.at[0]),
                (k_in, k),
                (v_in, v),
                (x_in, x5),
                (wa_in.at[1], w.at[1]),
                (wa_in.at[2], w.at[2]),
                (wa_in.at[0], w.at[0]),
            )
        )
    ]
    for copy in loads[:-1]:
        copy.start()
    feed.start()
    fill_mask(q_seg, k_seg, mask)
    branch[...] = grad_res[...].astype(BF)
    loads[0].wait()
    g[...] = dot(branch[...], w[0], NT).astype(BF)
    loads[-1].start()
    loads[1].wait()
    loads[2].wait()
    pairs = padded // LANES

    def some(begin, end):
        @pl.loop(begin, end)
        def _(i):
            at = pl.ds(pl.multiple_of(i * LANES, LANES), LANES)
            one, two, three = attend_back_pair(q[:, at], k[:, at], v[:, at], g[:, at], lse[i], mask)
            dq[:, at] = one
            dk[:, at] = two
            dv[:, at] = three

    order = feed.order()
    third, most = pairs // 3, len(order)
    some(0, third)
    for d in order[: most // 2]:
        feed.to_first(d)
    some(third, 2 * third)
    for d in order[most // 2 : most - 1]:
        feed.to_first(d)
    some(2 * third, pairs)
    for d in order[most - 1 :]:
        feed.to_first(d)
    for copy in loads[3:]:
        copy.wait()
    sums[...] = sums_in[...]

    def input_part(j, extra_part):
        at = pl.ds(j * rows, rows)
        grad = dot(dk[at, :], w[1], NN) + dot(dv[at, :], w[2], NN)
        if extra_part:
            grad = grad + dot(dq[...], w[0], NN)
        normed, scale = normed_rows(x5[at, :].astype(F32), width)
        sums[0:1] += jnp.sum(grad * normed, 0, keepdims=True)
        sums[1:2] += jnp.sum(grad, 0, keepdims=True)
        back = norm_back(grad, normed, scale, vec[0:1], width)
        if extra_part:
            back = back + grad_res[...]
        store_packed(pg, (j,), back, main, rem)

    @pl.loop(0, span // rows - 1)
    def _(j):
        input_part(j, False)

    input_part(span // rows - 1, True)
    for d in order:
        feed.to_z(d)
    feed.close()
    feed.finish()


def backward(grad_res, q, lse, q_seg, k_seg, vec, sums, k, v, wa, x5, pm, rem):
    wide = pm.shape[0]
    outer = wide // 2
    rows, padded = q.shape
    span = k.shape[0]
    main = pm.shape[3]
    block = pm.shape[2:]
    vmem = pl.BlockSpec(memory_space=pltpu.VMEM)
    shape = jax.ShapeDtypeStruct
    tokens = (rows + rem_rows(rows, main + rem), main)
    return pl.pallas_call(
        functools.partial(backward_kernel, outer, rem),
        out_shape=(
            shape((2,) + block, F32),
            shape((rows, padded), BF),
            shape((span, padded), BF),
            shape((span, padded), BF),
            shape((2, span // rows) + tokens, BF),
            shape((rows, padded), BF),
            shape(sums.shape, F32),
        ),
        in_specs=[vmem] * 7 + [ANY] * 5,
        out_specs=(vmem,) * 7,
        scratch_shapes=[
            pltpu.VMEM((3, padded, padded), BF),
            pltpu.VMEM((span, padded), BF),
            pltpu.VMEM((span, padded), BF),
            pltpu.VMEM((span, padded), BF),
            pltpu.VMEM((rows, padded), BF),
            pltpu.VMEM((span, rows), F32),
            pltpu.VMEM(block, BF),
        ]
        + scatter_scratch(outer, block)
        + [DMA((7,)), DMA]
        + scatter_sems(outer),
        compiler_params=pltpu.CompilerParams(
            collective_id=3, has_side_effects=True, vmem_limit_bytes=LIMIT
        ),
    )(grad_res, q, lse, q_seg, k_seg, vec, sums, k, v, wa, x5, pm)


def shards(
    layer_input,
    doc_segments,
    first_gain,
    first_shift,
    heads_weight,
    query_bias,
    value_bias,
    merge_weight,
    merge_bias,
    second_gain,
    second_shift,
    up_weight,
    up_bias,
    down_weight,
    down_bias,
    out_cotangent,
):
    parts = lax.axis_size("narrow")
    wide = lax.axis_size("wide")
    c, w, n = lax.axis_index("dp"), lax.axis_index("wide"), lax.axis_index("narrow")
    half = heads_weight.shape[0]
    width = half * parts
    padded = -(-width // LANES) * LANES
    cols = heads_weight.shape[2]
    units = up_weight.shape[1]
    hc, fc = cols // 2, up16(units // 2)
    short = fc - units // 2
    rows = layer_input.shape[0] // parts
    span = (REACH + 1) * rows

    by_half = heads_weight.transpose(1, 2, 0).reshape(3, 2, hc, half)
    heads_rows = lax.dynamic_index_in_dim(by_half, c, 1, False).reshape(3 * hc, half)
    merge_rows = lax.dynamic_slice_in_dim(merge_weight, c * hc, hc, 0)
    up_rows = lax.dynamic_slice_in_dim(up_weight, c * (units // 2), units // 2, 1).T
    down_rows = lax.dynamic_slice_in_dim(down_weight, c * (units // 2), units // 2, 0)
    up_rows = jnp.pad(up_rows, ((0, short), (0, 0)))
    down_rows = jnp.pad(down_rows, ((0, short), (0, 0)))
    line = lambda *v: jnp.pad(jnp.concatenate(v), (0, half - sum(e.shape[0] for e in v)))
    vectors = jnp.stack([first_gain, first_shift, merge_bias, second_gain, second_shift, down_bias])
    gap = up16(4 * hc) - 4 * hc
    sa = jnp.concatenate([heads_rows, merge_rows, jnp.zeros((gap, half), BF), vectors, jnp.zeros((10, half), BF)], 0)
    part = lambda v, size: lax.dynamic_slice_in_dim(v, c * size, size, 0)
    zero = lambda size: jnp.zeros((size,), BF)
    unit = jnp.array([0, 1, 0, 0, 1, 0], BF)
    column_a = jnp.concatenate(
        [part(query_bias, hc), zero(hc), part(value_bias, hc), zero(hc + gap), unit, zero(10)]
    )
    sm = jnp.concatenate([up_rows, down_rows], 0)
    column_m = jnp.concatenate([part(up_bias, units // 2), zero(short + fc)])
    xin = pack(layer_input.reshape(2, rows, half))
    cot_in = pack(out_cotangent.reshape(2, rows, half))
    seg_row = lax.dynamic_index_in_dim(doc_segments, c, 0, keepdims=False)
    start = (w * parts + n) * rows
    ahead = jnp.concatenate([jnp.full((REACH * rows,), -1, jnp.int32), seg_row])
    k_seg = lax.dynamic_slice_in_dim(ahead, start, span, 0)[:, None]
    q_seg = lax.dynamic_slice_in_dim(seg_row, start, rows, 0)[None]

    rem = widths(half)[1]
    cot_all, gm, wa, x5, low1, key, value, query, mixed, lse, residual, low2, vec = forward(
        xin, cot_in, pack(sa, column_a), pack(sm, column_m), q_seg, k_seg, hc, rem
    )
    pm, lo, grad_residual, sums = mlp(low2, cot_all, gm, residual, vec, fc, rem)

    mo, dq, dk, dv, pg, branch, sums = backward(
        grad_residual, query, lse, q_seg, k_seg, vec, sums, key, value, wa, x5, pm, rem
    )
    ao, xg, lo_out, sums = leave(dq, dk, dv, low1, mixed, branch, sums, pg, lo, hc, rem)

    layer_output = unpack_half(lo_out, rows, half).reshape(2 * rows, half)
    input_grad = unpack_half(xg, rows, half).reshape(2 * rows, half)
    biases = column_of(ao, up16(4 * hc), half)
    ao = unpack_half(ao, up16(4 * hc), half)
    heads_total = ao[:, : 3 * hc].reshape(2, 3, hc, half).transpose(3, 1, 0, 2).reshape(half, 3, cols)
    merge_total = ao[:, 3 * hc : 4 * hc].reshape(cols, half)
    up_bias_total = column_of(mo, 2 * fc, half)[:, : units // 2].reshape(units)
    mo = unpack_half(mo, 2 * fc, half)
    up_total = mo[:, : units // 2].reshape(units, half).T
    down_total = mo[:, fc : fc + units // 2].reshape(units, half)

    lines = lax.dynamic_index_in_dim(halves(sums[:6, :width]), n, 0, False)
    query_total = biases[:, :hc].reshape(cols)
    value_total = biases[:, 2 * hc : 3 * hc].reshape(cols)
    return (
        layer_output,
        input_grad,
        lines[0],
        lines[1],
        heads_total,
        query_total,
        value_total,
        merge_total,
        lines[2],
        lines[3],
        lines[4],
        up_total,
        up_bias_total,
        down_total,
        lines[5],
    )


def solution(mesh):
    return jax.shard_map(
        shards,
        mesh=mesh,
        in_specs=(
            P(("dp", "wide"), "narrow"),
            P(),
            P("narrow"),
            P("narrow"),
            P("narrow", None, "wide"),
            P("wide"),
            P("wide"),
            P("wide", "narrow"),
            P("narrow"),
            P("narrow"),
            P("narrow"),
            P("narrow", "wide"),
            P("wide"),
            P("wide", "narrow"),
            P("narrow"),
            P(("dp", "wide"), "narrow"),
        ),
        out_specs=(
            P(("dp", "wide"), "narrow"),
            P(("dp", "wide"), "narrow"),
            P("narrow"),
            P("narrow"),
            P("narrow", None, "wide"),
            P("wide"),
            P("wide"),
            P("wide", "narrow"),
            P("narrow"),
            P("narrow"),
            P("narrow"),
            P("narrow", "wide"),
            P("wide"),
            P("wide", "narrow"),
            P("narrow"),
        ),
        check_vma=False,
    )
```

time: 814 us -> 517 us (0.64)
  local copies, waits for them, and re-layouts: 187 us -> 38.7 us
  other arithmetic: 74.8 us -> 7.22 us
  matrix products: 51 us -> 0 us
  blocking collectives: 48 us -> 0 us
  Pallas kernels: 443 us -> 459 us
    dot_general x12 -> x0, matrix products: 51 us -> none  [dot(): lax.dot_general(left, right, ((dims[0], dims[1]), ((), ())), preferred_el...]
    psum x1 -> x0, blocking collectives: 48 us -> none  [shards(): lax.psum((lines, jnp.sum(dq, 0, dtype=F32)[:width], jnp.sum(dv, 0, dtype=...]
    reshape x7 -> x9, local copies, waits for them, and re-layouts: 23.3 us -> 2.51 us  [the longest x1 0.68 us: shards(): up_bias_total = column_of(mo, 2 * fc, half)[:, :units // 2].reshape(units)]
    concatenate x2, local copies, waits for them, and re-layouts: 22 us -> 1.55 us  [the longest x1 0.79 us: shards(): jnp.concatenate([heads_rows, merge_rows, jnp.zeros((gap, half), BF), vect...]
    slice x13 -> x6, local copies, waits for them, and re-layouts: 19 us -> 0.24 us  [the longest x4 0.16 us: pack(): tail = jnp.concatenate([tail[:, :base], column, tail[:, base + groups:]], 1)]
    transpose x4, local copies, waits for them, and re-layouts: 18.2 us -> 1.05 us  [column_of(): jnp.swapaxes(tail, -1, -2).reshape(block.shape[:-2] + (groups * extra,))]
    transpose x2 -> x0, other arithmetic: 16.8 us -> none  [the longest x1 9.72 us: shards(): pa = jnp.moveaxis(pack(halves(pa)), 0, 2)]
    reduce_sum x6 -> x0, other arithmetic: 16.3 us -> none  [the longest x1 5.84 us: norm_backward(): return (back, jnp.sum(grad * normed, 0), jnp.sum(grad, 0))]
where the time goes in v2:
time: 517 us; the launch traced here: 507 us
  Pallas kernels  459 us (89%)
  local copies, waits for them, and re-layouts  38.7 us (7%)
  other arithmetic  7.22 us (1%)
    pallas_call x1, Pallas kernels, forward(): pl.pallas_call(functools.partial(forward_kernel, outer, hc, rem), out_sha...  158 us
    pallas_call x1, Pallas kernels, backward(): pl.pallas_call(functools.partial(backward_kernel, outer, rem), out_shape=...  126 us
    pallas_call x1, Pallas kernels, leave(): pl.pallas_call(functools.partial(leave_kernel, outer, hc, rem), out_shape...  124 us
    pallas_call x1, Pallas kernels, mlp(): pl.pallas_call(functools.partial(mlp_kernel, wide, fc, rem), out_shape=(j...  50.9 us

profile of v2, /device:TPU:11, one launch (start us, length us, event | category | flops | bytes accessed | tf_op | source)
XLA Modules:
  0.0 506.7 jit_solution(1570335031103993078)
XLA Ops:
  0.7 1.4 dynamic_slice.43.q_seg
  2.1 0.7 dynamic_slice.38
  2.9 0.7 dynamic_slice.39
  3.6 0.8 concatenate.64
  4.4 0.8 dynamic_slice.42
  5.2 0.7 stack.27
  5.9 0.7 stack.28
  6.6 0.7 stack.29
  7.3 0.7 stack.30
  8.0 0.7 stack.31
  8.6 0.7 stack.32
  9.5 0.1 copy.56
  9.6 0.8 constant_dynamic-slice_fusion
  10.5 0.9 constant_dynamic-slice_fusion.3
  11.5 0.2 constant_dynamic-slice_fusion.2
  11.7 0.2 copy.72
  12.1 0.2 reshape.157
  12.4 0.9 maximum_maximum_fusion.sm
  13.3 0.1 reshape.151
  13.5 0.8 concatenate.63
  14.4 0.2 reshape.154
  14.7 0.8 maximum_maximum_fusion.1.sa
  15.5 1.1 broadcast_in_dim.11.k_seg
  16.6 0.3 copy.48
  17.0 0.2 reshape.147
  17.1 0.5 copy-done.6
  17.6 0.3 copy.50
  18.0 0.2 reshape.150
  18.2 1.1 pad_maximum_fusion.1
  19.2 157.8 %shard_map.280 = (bf16[2,2,272,512]{3,2,1,0:T(8,128)(2,1)}, bf16[8,2,592,512]{3,2,1,0:T(8,128)(2,1)}, bf16[4,1152,1152]{2,1,0:T(8,128)(2,1)}, bf16[1280,1152]{1,...) custom-call(bf16[2,272,512]{2,1,0:T(8,128)(2,1)} %get-tuple-element., ...), custom_call_target="tpu_custom_call" | custom-call | tf_op jit(solution)/shard_map/pallas_call | solution.py:927
  177.1 50.9 %shard_map.281 = (bf16[8,2,592,512]{3,2,1,0:T(8,128)(2,1)}, bf16[2,272,512]{2,1,0:T(8,128)(2,1)}, f32[256,1152]{1,0:T(8,128)}, f32[16,1152]{1,0:T(8,128)}) custom-call(bf16[256,1152]{1,0:T(8,128)(2,1)} %get-tuple-element.43.low2, bf16[2,2,272,512]{3,2,1,0:T(8,128)(2,1)} %get-tuple-element.44.cot_in, bf16[8,2,592,512]{3,2,1,0:T(8,128)(2,1)} %get-tuple-element.45.gm, ...), custom_call_target="tpu_custom_call" | custom-call | tf_op jit(solution)/shard_map/pallas_call | solution.py:684
  228.0 126.3 %shard_map.282 = (f32[2,592,512]{2,1,0:T(8,128)}, bf16[256,1152]{1,0:T(8,128)(2,1)}, bf16[1280,1152]{1,0:T(8,128)(2,1)}, bf16[1280,1152]{1,0:T(8,128)(2,1)}, bf1...) custom-call(f32[256,1152]{1,0:T(8,128)} %get-tuple-element.48.grad_res, ...), custom_call_target="tpu_custom_call" | custom-call | tf_op jit(solution)/shard_map/pallas_call | solution.py:1091
  354.3 124.2 %shard_map.283 = (f32[2,304,512]{2,1,0:T(8,128)}, bf16[2,272,512]{2,1,0:T(8,128)(2,1)}, bf16[2,272,512]{2,1,0:T(8,128)(2,1)}, f32[16,1152]{1,0:T(8,128)}) custom-call(bf16[256,1152]{1,0:T(8,128)(2,1)} %get-tuple-element.57.dq, bf16[1280,1152]{1,0:T(8,128)(2,1)} %get-tuple-element.58.dk, bf16[1280,1152]{1,0:T(8,128)(2,1)} %get-tuple-element.59.dv, ...), custom_call_target="tpu_custom_call" | custom-call | tf_op jit(solution)/shard_map/pallas_call | solution.py:470
  478.5 0.8 fusion.8
  479.3 0.8 fusion.7
  480.2 0.6 slice_reduce_fusion
  480.8 0.8 slice.152
  481.6 1.1 slice.151
  482.7 0.2 copy.60
  482.9 0.2 copy.63
  483.2 1.0 copy-done.4
  484.5 0.7 reshape.167
  485.1 0.6 reshape.166
  485.8 0.8 slice_bitcast_fusion
  486.8 0.7 reshape.173
  487.4 0.1 reshape.160
  487.7 0.8 pad_maximum_fusion.4
  488.6 0.1 reshape.159
  488.8 0.8 pad_maximum_fusion.3
  489.7 0.7 slice.162
  490.4 1.1 slice.173
  491.5 0.6 copy-done.2
  492.1 0.2 slice.172
  492.3 1.9 reshape.161
  494.2 1.2 copy.65
  495.4 0.8 pad_maximum_fusion.5
  496.3 1.5 copy.66
  497.8 0.8 reshape.168
  498.5 1.3 copy.67
  499.8 1.1 reshape.164
  500.9 0.2 reshape.169
  501.1 0.2 copy.69
  501.4 1.8 pad_maximum_fusion
  503.2 3.0 copy.70
  (65 shorter events, 2.1 us)
Async XLA Ops:
  0.6 10.8 %copy-start = (bf16[544,544]{1,0:T(8,128)(2,1)S(1)}, bf16[544,544]{1,0:T(8,128)(2,1)}, u32[]{:S(2)}) copy-start(bf16[544,544]{1,0:T(8,128)(2,1)} %param.30) | copy-start | bytes 1775620
  0.7 10.8 %copy-start.9 = (bf16[544,544]{1,0:T(8,128)(2,1)S(1)}, bf16[544,544]{1,0:T(8,128)(2,1)}, u32[]{:S(2)}) copy-start(bf16[544,544]{1,0:T(8,128)(2,1)} %param.28) | copy-start | bytes 1775620
  12.0 1.3 copy-start.8
  14.3 2.3 copy-start.5
  16.6 1.1 copy-start.6
  479.3 3.5 copy-start.7
  482.9 1.3 copy-start.4
  490.3 1.8 copy-start.2
  496.3 1.5 copy-start.3
  503.2 3.0 copy-start.1
